TPU v7x, 128 devices: a whole 4x4x4 slice. The times are simulated.
128 devices in a mesh: cells: 16 (over z, y_lo, core), snap: 8 (over y_hi, x).
Axes of the slice: x: 4, y: 4 (y_hi: 2, y_lo: 2; y = y_hi * 2 + y_lo), z: 4, core: 2. Of those that a mesh axis runs over, the one named last changes fastest.
Arguments:
- snapshots: bfloat16 [4096, 65536], P('snap', 'cells'), may hold values from -8 to 8
- pod_basis: bfloat16 [96, 65536], P(None, 'cells'), may hold values from -0.0234375 to 0.0234375
- reference_field: bfloat16 [65536], P('cells'), may hold values from -6 to 6
- ridge_weights: float32 [4752], replicated, may hold values from 0.2 to 2
Outputs:
- trailing_gram: float32 [4752, 4752], P('cells', 'snap')
- panel_factor: float32 [4752, 512], P('cells')
All inputs are finite; a program needn't handle non-finite values.
Results may differ from a plain program's by a relative error of at most 0.0003.
Values sent between devices are 32-bit elements; how exact they have to be, the bound alone decides.
No kernel may reach another device: no remote copies, remote signals or barrier semaphores. Data moves between devices by JAX's collectives and lax.ppermute only.
A program may use at most 128 MiB of HBM per device.

v0:
```python
import functools
import math

import jax
import jax.numpy as jnp
import numpy as np
from jax import lax
from jax.experimental import pallas as pl
from jax.experimental.pallas import tpu as pltpu
from jax.sharding import PartitionSpec as P

PANEL = 512
HI = lax.Precision.HIGHEST
HALF = 256
BLOCK = 128
STEP = 32
SLOTS = 112
F32 = jnp.float32
BF16 = jnp.bfloat16
NT = (((1,), (1,)), ((), ()))
TN = (((0,), (0,)), ((), ()))
NN = (((1,), (0,)), ((), ()))


def dot(a, b, dims, precision=None):
    return lax.dot_general(a, b, dims, precision=precision, preferred_element_type=F32)


def split(value):
    high = value.astype(BF16)
    return high, (value - high.astype(F32)).astype(BF16)


def dot3(a, b):
    ah, al = a
    bh, bl = b
    return dot(jnp.concatenate([ah, ah, al], 1), jnp.concatenate([bh, bl, bh], 1), NT)


def pick_tables(first, rows, modes):
    index = first + lax.broadcasted_iota(jnp.int32, (rows, 128), 0)
    slot = lax.broadcasted_iota(jnp.int32, (rows, 128), 1)

    def offset(a):
        return modes + modes * a - (a * (a - 1)) // 2

    linear = index < modes
    here = (index >= offset(slot)) & (index < offset(slot + 1)) & (slot < modes)
    right_value = jnp.where(here, index - offset(slot) + slot, 0).astype(F32)
    right_index = jnp.sum(right_value, axis=1, keepdims=True).astype(jnp.int32)
    left_index = jnp.sum(jnp.where(here, slot, 0).astype(F32), axis=1, keepdims=True).astype(jnp.int32)
    left_index = jnp.where(linear, index, left_index)
    right_index = jnp.where(linear, modes, right_index)
    return (slot == left_index).astype(F32), (slot == right_index).astype(F32)


def pick_kernel(modes, scale, scal, lr, rr, lc, rc):
    for ref_l, ref_r, first in ((lr, rr, scal[0]), (lc, rc, scal[1])):
        block = math.gcd(lr.shape[0], ref_l.shape[0])

        def rows_body(i, carry, ref_l=ref_l, ref_r=ref_r, first=first):
            at = pl.ds(pl.multiple_of(i * block, 16), block)
            left, right = pick_tables(first + i * block, block, modes)
            for ref, value in ((ref_l, left * scale), (ref_r, right)):
                ref[at, 0:SLOTS] = value[:, 0:SLOTS].astype(BF16)
                ref[at, SLOTS : 2 * SLOTS] = value[:, 0:SLOTS].astype(BF16)
            return carry

        lax.fori_loop(0, ref_l.shape[0] // block, rows_body, 0)


def picks(scal, row_pad, col_pad, modes, scale):
    shapes = [(row_pad, 2 * SLOTS)] * 2 + [(col_pad, 2 * SLOTS)] * 2
    return pl.pallas_call(
        functools.partial(pick_kernel, modes, scale),
        in_specs=[pl.BlockSpec(memory_space=pltpu.SMEM)],
        out_shape=[jax.ShapeDtypeStruct(s, BF16) for s in shapes],
        compiler_params=pltpu.CompilerParams(vmem_limit_bytes=40 * 2**20),
        name="picks",
    )(scal)


def panel_features(c_ref, t, f_ref, modes, scale):
    f_ref[0:modes, :] = c_ref[t] * scale
    at, a = modes, 0
    while at < PANEL:
        count = min(modes - a, PANEL - at)
        f_ref[at : at + count, :] = c_ref[t, a : a + count, :] * (c_ref[t, a : a + 1, :] * scale)
        at += count
        a += 1


def panel_pair(t, c_s, f_s, fh, fl, modes, scale):
    for i in range(2):
        panel_features(c_s, t + i, f_s.at[i], modes, scale)
        fh[t + i], fl[t + i] = split(f_s[i])


def corner_pair(t, fh, fl, a_ref):
    pairs = [(fh[t + i], fl[t + i]) for i in range(2)]
    top = [dot3((h[0:HALF], l[0:HALF]), (h, l)) for h, l in pairs]
    low = [dot3((h[HALF:], l[HALF:]), (h[HALF:], l[HALF:])) for h, l in pairs]
    a_ref[0:HALF, :] = top[0] + top[1]
    a_ref[HALF:, HALF:] = low[0] + low[1]


def lane_bcast(x, c):
    return jnp.broadcast_to(x[:, c : c + 1], (8, 128))


def sub_bcast(x, k):
    return jnp.broadcast_to(x[k : k + 1, :], (8, 128))


def split3(value):
    high = value.astype(BF16)
    rest = value - high.astype(F32)
    middle = rest.astype(BF16)
    return high, middle, (rest - middle.astype(F32)).astype(BF16)


def update_dot(left, right):
    lh, lm, ll = split3(left)
    rh, rm, rl = split3(right)
    return dot(
        jnp.concatenate([lh, lh, lh, lm, lm, ll], 0), jnp.concatenate([rh, rm, rl, rh, rm, rh], 0), TN
    )


def factor_step(s_ref, b, between):
    lo = STEP * b
    strips = STEP // 8
    sub = lax.broadcasted_iota(jnp.int32, (8, 128), 0)
    T = [[s_ref[lo + 8 * r : lo + 8 * r + 8, 0:128], s_ref[lo + 8 * r : lo + 8 * r + 8, 128:256]] for r in range(strips)]
    B = {(r, j): lane_bcast(T[r][0], lo + j) for j in range(STEP) for r in range(j // 8, strips)}
    for q in range(strips):
        scale = None
        for k in range(8 * q, 8 * q + 8):
            rs = lax.rsqrt(sub_bcast(B[q, k], k - 8 * q))
            inv = rs * rs
            scale = rs if scale is None else jnp.where(sub == k - 8 * q, rs, scale)
            row = [sub_bcast(part, k - 8 * q) for part in T[q]]
            pivots = {j: sub_bcast(B[j // 8, k], j % 8) for j in range(k + 1, STEP)}
            for r in range(q, strips):
                m = B[r, k] * inv
                if r == q:
                    m = jnp.where(sub > k - 8 * q, m, 0.0)
                for j in range(k + 1, STEP):
                    if j // 8 <= r:
                        B[r, j] = B[r, j] - m * pivots[j]
                T[r] = [part - m * line for part, line in zip(T[r], row)]
        T[q] = [part * scale for part in T[q]]
        between(4 * b + q)
    for r in range(strips):
        s_ref[lo + 8 * r : lo + 8 * r + 8, 0:128] = T[r][0]
        s_ref[lo + 8 * r : lo + 8 * r + 8, 128:256] = T[r][1]
    if b < 3:
        full = s_ref[lo : lo + STEP, :]
        upd = update_dot(full[:, 0:128], full)
        s_ref[lo + STEP : 128, :] -= upd[lo + STEP :, :]


def factor_block(k, a_s, s_ref, e_s, u_s, inv_s, low_s, between):
    lo, hi = BLOCK * k, BLOCK * (k + 1)
    ri = lax.broadcasted_iota(jnp.int32, (BLOCK, BLOCK), 0)
    ci = lax.broadcasted_iota(jnp.int32, (BLOCK, BLOCK), 1)
    s_ref[:, 0:BLOCK] = a_s[lo:hi, lo:hi]
    s_ref[:, BLOCK:] = (ri == ci).astype(F32)
    for b in range(4):
        factor_step(s_ref, b, between)
    inverse = s_ref[:, BLOCK:]
    inv_s[k] = inverse
    if hi < PANEL:
        rest = dot(inverse, a_s[lo:hi, hi:], NN, HI)
        u_s[lo:hi, hi:] = rest
        a_s[hi : hi + BLOCK, hi:] -= dot(rest[:, 0:BLOCK], rest, TN, HI)
        if hi + BLOCK < PANEL:
            far = rest[:, BLOCK:]
            a_s[hi + BLOCK :, hi + BLOCK :] -= dot(far, far, TN, HI)
    if k % 2:
        low_s[k // 2] = dot(inverse, e_s[...], NN, HI)
    else:
        e_s[...] = -dot(rest[:, 0:BLOCK], inverse, TN, HI)


def stacked(c, modes):
    n = c.shape[1]
    high, low = split(c)
    gap = lax.broadcasted_iota(jnp.int32, (SLOTS - modes, n), 0)
    ones = (gap == 0).astype(F32).astype(BF16)
    none = jnp.zeros((SLOTS - modes, n), BF16)
    return jnp.concatenate([high, ones, low, none], axis=0)


def picked(left, right, cs):
    return split(dot(left, cs, NN) * dot(right, cs, NN))


def block_parts(t, c_s, fh, fl, lr, rr, lc, rc, gr, gc, gt, modes):
    env = {}

    def part0():
        cs = stacked(c_s[t], modes)
        env["fr"] = picked(lr[...], rr[...], cs)
        env["fc"] = picked(lc[...], rc[...], cs)
        env["fp"] = (fh[t], fl[t])

    def part1():
        gr[...] += dot3(env["fr"], env["fp"])

    def part2():
        gc[...] += dot3(env["fc"], env["fp"])

    def part3():
        gt[...] += dot3(env["fr"], env["fc"])

    return [part0, part1, part2, part3]


def pair_inverse(p, inv_s, low_s):
    zero = jnp.zeros((BLOCK, BLOCK), F32)
    top = jnp.concatenate([inv_s[2 * p], zero], 1)
    return jnp.concatenate([top, jnp.concatenate([low_s[p], inv_s[2 * p + 1]], 1)], 0)


def diagonal(shape, first_row, first_col, values):
    ri = first_row + lax.broadcasted_iota(jnp.int32, shape, 0)
    ci = first_col + lax.broadcasted_iota(jnp.int32, shape, 1)
    return jnp.where(ri == ci, values, 0.0)


def diagonal(shape, first_row, first_col, values):
    ri = first_row + lax.broadcasted_iota(jnp.int32, shape, 0)
    ci = first_col + lax.broadcasted_iota(jnp.int32, shape, 1)
    return jnp.where(ri == ci, values, 0.0)


def early_kernel(modes, scale, first, *refs):
    own, oth, lr, rr, lc, rc = refs[0:6]
    if first:
        scal, ridge_panel, ridge_cols = refs[6:9]
        a_out, gr, gc, gt, c_s, f_s, fh, fl, a_s, pair_s = refs[9:]
        pair_s[...] = jnp.zeros_like(pair_s)
        gc[...] = diagonal(gc.shape, scal[1], 0, ridge_panel[...])
        gt[...] = diagonal(gt.shape, scal[0], scal[1], ridge_cols[...])
    else:
        left, gr_in, gc_in, gt_in = refs[6:10]
        a_out, gr, gr_oth, gc, gt, c_s, f_s, fh, fl, a_s, pair_s = refs[10:]
        gc[...] = gc_in[...]
        gt[...] = gt_in[...]
        pair_s[...] = jnp.zeros_like(pair_s)
        for i in range(2):
            c_s[4 + i] = left[i]
        panel_pair(4, c_s, f_s, fh, fl, modes, scale)
    for i in range(2):
        c_s[i] = own[i]
        c_s[2 + i] = oth[i]

    def corner_body(i, carry):
        panel_pair(2 * i, c_s, f_s, fh, fl, modes, scale)
        corner_pair(2 * i, fh, fl, a_s.at[i])
        return carry

    if first:
        corner_body(0, 0)
        corner_body(1, 0)
    else:
        lax.fori_loop(0, 2, corner_body, 0)
    a_out[...] = a_s[0] + a_s[1]

    def pair_body(i, carry):
        for t in (2 * i, 2 * i + 1):
            for part in block_parts(t, c_s, fh, fl, lr, rr, lc, rc, pair_s.at[i], gc, gt, modes):
                part()
        return carry

    if first:
        pair_body(0, 0)
        gr[...] = pair_s[0]
    else:
        lax.fori_loop(0, 3, pair_body, 0)
        gr[...] = gr_in[...] + pair_s[0]
        gr_oth[...] = pair_s[2] + pair_s[1]


def early(own, oth, tables, rest, first, modes, scale, cost):
    lr, rr, lc, rc = tables
    row_pad, col_pad = lr.shape[0], lc.shape[0]
    n = own.shape[2]
    vmem = pl.BlockSpec(memory_space=pltpu.VMEM)
    smem = pl.BlockSpec(memory_space=pltpu.SMEM)
    held = 4 if first else 6
    scratch = [
        pltpu.VMEM((held, modes, n), F32),
        pltpu.VMEM((2, PANEL, n), F32),
        pltpu.VMEM((held, PANEL, n), BF16),
        pltpu.VMEM((held, PANEL, n), BF16),
        pltpu.VMEM((2, PANEL, PANEL), F32),
        pltpu.VMEM((1 if first else 3, row_pad, PANEL), F32),
    ]
    shapes = [(PANEL, PANEL)] + [(row_pad, PANEL)] * (1 if first else 2) + [(col_pad, PANEL), (row_pad, col_pad)]
    return pl.pallas_call(
        functools.partial(early_kernel, modes, scale, first),
        in_specs=[vmem] * 6 + ([smem, vmem, vmem] if first else [vmem] * 4),
        out_specs=[vmem] * len(shapes),
        out_shape=[jax.ShapeDtypeStruct(s, F32) for s in shapes],
        scratch_shapes=scratch,
        compiler_params=pltpu.CompilerParams(vmem_limit_bytes=32 * 2**20),
        cost_estimate=pl.CostEstimate(flops=cost, bytes_accessed=2**22, transcendentals=0),
        name="early_first" if first else "early_second",
    )(own, oth, lr, rr, lc, rc, *rest)


def corner_kernel(modes, scale, c_ref, a_out, fh, fl, f_s):
    for i in range(2):
        panel_pair(2 * i, c_ref, f_s, fh, fl, modes, scale)
        corner_pair(2 * i, fh, fl, a_out.at[i])


def corner_of(own, modes, scale):
    n = own.shape[2]
    vmem = pl.BlockSpec(memory_space=pltpu.VMEM)
    return pl.pallas_call(
        functools.partial(corner_kernel, modes, scale),
        in_specs=[vmem],
        out_specs=[vmem] * 3,
        out_shape=[
            jax.ShapeDtypeStruct((2, PANEL, PANEL), F32),
            jax.ShapeDtypeStruct((4, PANEL, n), BF16),
            jax.ShapeDtypeStruct((4, PANEL, n), BF16),
        ],
        scratch_shapes=[pltpu.VMEM((2, PANEL, n), F32)],
        compiler_params=pltpu.CompilerParams(vmem_limit_bytes=24 * 2**20),
        cost_estimate=pl.CostEstimate(flops=10**9, bytes_accessed=2**22, transcendentals=0),
        name="late_corner",
    )(own)


def halves_kernel(core_ref, part, offset, keep, send):
    core = core_ref[0]
    half = keep.shape[1]
    mine = pl.multiple_of(core * half, half)
    other = pl.multiple_of((1 - core) * half, half)
    send[...] = (part[pl.ds(other, half), :] - offset[...]).T
    keep[...] = (part[pl.ds(mine, half), :] - offset[...]).T


def halves(core, part, offset):
    vmem = pl.BlockSpec(memory_space=pltpu.VMEM)
    snaps, modes = part.shape
    return pl.pallas_call(
        halves_kernel,
        in_specs=[pl.BlockSpec(memory_space=pltpu.SMEM)] + [vmem] * 2,
        out_specs=[vmem] * 2,
        out_shape=[jax.ShapeDtypeStruct((modes, snaps // 2), F32)] * 2,
        compiler_params=pltpu.CompilerParams(vmem_limit_bytes=16 * 2**20),
        name="halves",
    )(core, part, offset)


LATE = 8


def main_kernel(modes, scale, scal, own, oth, lr, rr, lc, rc, ridge_panel,
                own_h, own_l, a_own, a0, a1, gr_in, gr_oth_in, gc_in, gt_in,
                tile_out, rows_out,
                f_s, fh, fl, a_p, a_s, s_s, e_s, u_s, inv_s, low_s, gr, gc, gt, pr, pc):
    first_row, first_col = scal[0], scal[1]
    rows, cols = tile_out.shape

    def corner_body(i, carry):
        panel_pair(2 * i, oth, f_s, fh, fl, modes, scale)
        corner_pair(2 * i, fh, fl, a_p.at[i])
        return carry

    lax.fori_loop(0, 2, corner_body, 0)
    total = (a0[...] + a1[...]) + ((a_own[0] + a_p[0]) + (a_own[1] + a_p[1]))
    a_s[...] = total + diagonal(a_s.shape, 0, 0, ridge_panel[...])
    gr[...] = jnp.zeros_like(gr)
    gc[...] = gc_in[...]
    gt[...] = gt_in[...]

    parts = []
    for t in range(LATE):
        held = (own, own_h, own_l) if t < 4 else (oth, fh, fl)
        parts += block_parts(t % 4, *held, lr, rr, lc, rc, gr.at[t // 2], gc, gt, modes)

    def solve_first():
        inverse = pair_inverse(0, inv_s, low_s)
        cross = u_s[0:HALF, HALF:]
        line = diagonal(pr.shape, first_row, 0, ridge_panel[...])
        sums = (gr_in[...] + (gr[0] + gr[1])) + (gr_oth_in[...] + (gr[2] + gr[3])) + line
        for p, g in ((pr, sums), (pc, gc[...])):
            first = dot(g[:, 0:HALF], inverse, NT, HI)
            p[:, 0:HALF] = first
            p[:, HALF:] = g[:, HALF:] - dot(first, cross, NN, HI)

    def update(at):
        ri = first_row + lax.broadcasted_iota(jnp.int32, gt.shape, 0)
        ci = first_col + lax.broadcasted_iota(jnp.int32, gt.shape, 1)
        change = dot3(split(pr[:, at : at + HALF]), split(pc[:, at : at + HALF]))
        return gt[...] - jnp.where((ri >= PANEL) & (ci >= PANEL), change, 0.0)

    def write_rows(at):
        line = first_row + lax.broadcasted_iota(jnp.int32, (rows, HALF), 0)
        place = at + lax.broadcasted_iota(jnp.int32, (rows, HALF), 1)
        rows_out[:, at : at + HALF] = jnp.where(place <= line, pr[0:rows, at : at + HALF], 0.0)

    def update_first():
        gt[...] = update(0)
        write_rows(0)

    slots = [[] for _ in range(64)]
    for i, part in enumerate(parts):
        slots[i * 48 // len(parts)].append(part)
    slots[49].append(solve_first)
    slots[54].append(update_first)

    def between_of(k):
        def between(i):
            for part in slots[16 * k + i]:
                part()

        return between

    for k in range(4):
        factor_block(k, a_s, s_s, e_s, u_s, inv_s, low_s, between_of(k))

    inverse = pair_inverse(1, inv_s, low_s)
    for p in (pr, pc):
        p[:, HALF:] = dot(p[:, HALF:], inverse, NT, HI)
    tile_out[...] = update(HALF)[0:rows, 0:cols]
    write_rows(HALF)


def main(scal, own, oth, tables, ridge_panel, sums, rows, cols, scale):
    modes, n = own.shape[1:]
    lr, rr, lc, rc = tables
    row_pad, col_pad = lr.shape[0], lc.shape[0]
    vmem = pl.BlockSpec(memory_space=pltpu.VMEM)
    return pl.pallas_call(
        functools.partial(main_kernel, modes, scale),
        in_specs=[pl.BlockSpec(memory_space=pltpu.SMEM)] + [vmem] * 16,
        out_specs=[vmem, vmem],
        out_shape=[jax.ShapeDtypeStruct((rows, cols), F32), jax.ShapeDtypeStruct((rows, PANEL), F32)],
        scratch_shapes=[
            pltpu.VMEM((2, PANEL, n), F32),
            pltpu.VMEM((4, PANEL, n), BF16),
            pltpu.VMEM((4, PANEL, n), BF16),
            pltpu.VMEM((2, PANEL, PANEL), F32),
            pltpu.VMEM((PANEL, PANEL), F32),
            pltpu.VMEM((BLOCK, 2 * BLOCK), F32),
            pltpu.VMEM((BLOCK, BLOCK), F32),
            pltpu.VMEM((PANEL, PANEL), F32),
            pltpu.VMEM((4, BLOCK, BLOCK), F32),
            pltpu.VMEM((2, BLOCK, BLOCK), F32),
            pltpu.VMEM((LATE // 2, row_pad, PANEL), F32),
            pltpu.VMEM((col_pad, PANEL), F32),
            pltpu.VMEM((row_pad, col_pad), F32),
            pltpu.VMEM((row_pad, PANEL), F32),
            pltpu.VMEM((col_pad, PANEL), F32),
        ],
        compiler_params=pltpu.CompilerParams(vmem_limit_bytes=32 * 2**20),
        name="gram_factor",
    )(scal, own, oth, lr, rr, lc, rc, ridge_panel, *sums)


def swap(value, axis, bit, other_bit=None):
    size = lax.axis_size(axis)
    bits = (bit, bit if other_bit is None else other_bit)
    return lax.ppermute(value, axis, [(i, i ^ bits[i & 1]) for i in range(size)])


def padded(count):
    return -(-count // 16) * 16


def per_device(snapshots, pod_basis, reference_field, ridge_weights):
    modes = pod_basis.shape[0]
    snap_total = snapshots.shape[0] * lax.axis_size("snap")
    scale = snap_total**-0.5
    feature_total = ridge_weights.shape[0]
    rows = feature_total // lax.axis_size("cells")
    cols = feature_total // lax.axis_size("snap")
    group = lax.axis_index("snap")
    core = lax.axis_index("cells") & 1
    first_row = lax.axis_index("cells") * rows
    first_col = group * cols
    scal = jnp.stack([first_row, first_col]).astype(jnp.int32)
    tables = picks(scal, padded(rows), padded(cols), modes, scale)
    ridge_panel = ridge_weights[None, :PANEL]
    ridge_cols = lax.dynamic_slice_in_dim(ridge_weights, first_col, cols)
    ridge_cols = jnp.pad(ridge_cols, (0, padded(cols) - cols))[None, :]

    projected = lax.dot_general(snapshots, pod_basis, NT, preferred_element_type=F32)
    offset = lax.dot_general(reference_field[None, :], pod_basis, NT, preferred_element_type=F32)
    keep, send = halves(core[None].astype(jnp.int32), projected, offset)
    total = keep + swap(send, "cells", 1)
    for bit, other_bit in ((2, 4), (4, 2), (8, 8)):
        total = total + swap(total, "cells", bit, other_bit)

    together = lax.optimization_barrier
    own0 = total[None]
    own1 = swap(own0, "snap", 4)
    oth0 = swap(own0, "cells", 1)
    own1, oth0, tables, ridge_panel, ridge_cols = together((own1, oth0, tables, ridge_panel, ridge_cols))
    pair = jnp.concatenate([own0, own1], 0)
    own2 = swap(pair, "snap", 2)
    oth_pair = jnp.concatenate([oth0, swap(own1, "cells", 1)], 0)
    sums = early(pair, oth_pair, tables, (scal, ridge_panel, ridge_cols), True, modes, scale, 4 * 10**9)
    own2, a0, *sums = together((own2, *sums))
    own3 = swap(jnp.concatenate([pair, own2], 0), "snap", 1)
    oth2 = swap(own2, "cells", 1)
    sums = early(own2, oth2, tables, (oth_pair, *sums), False, modes, scale, 4 * 10**9)
    own3, a1, *sums = together((own3, *sums))
    oth3 = swap(own3, "cells", 1)
    a_own, own_h, own_l = corner_of(own3, modes, scale)
    oth3, a_own, own_h, own_l = together((oth3, a_own, own_h, own_l))
    given = (own_h, own_l, a_own, a0, a1, *sums)
    return tuple(main(scal, own3, oth3, tables, ridge_panel, given, rows, cols, scale))


def solution(mesh):
    return jax.shard_map(
        per_device,
        mesh=mesh,
        in_specs=(P("snap", "cells"), P(None, "cells"), P("cells"), P()),
        out_specs=(P("cells", "snap"), P("cells", None)),
        check_vma=False,
    )
```

profile of v0, /device:TPU:1, one launch (start us, length us, event | category | flops | bytes accessed | tf_op | source)
XLA Modules:
  0.0 81.4 jit_solution(18375665156993392670)
XLA Ops:
  0.7 0.8 reshape.7
  2.1 3.4 %fusion.part = f32[512,96]{1,0:T(8,128)S(1)} fusion(bf16[512,4096]{1,0:T(8,128)(2,1)} %param.4, bf16[96,4096]{1,0:T(8,128)(2,1)S(1)} %copy-done), kind=kOutput, calls=%fused_computation.6 | convolution fusion | flops 402653184 | bytes 5177344 | tf_op jit(solution)/shard_map/dot_general | solution.py:495
  5.7 1.5 %collective-permute-start = (f32[96,256]{1,0:T(8,128)S(1)}, f32[96,256]{1,0:T(8,128)S(1)}, u32[]{:S(2)}, u32[]{:S(2)}) collective-permute-start(f32[96,256]{1,0:T(8,128)S(1)} %get-tuple-element.44), channel_id=1, source_target_pairs={{0,8},{8,0},{16,24},{24,16},{32,40},{40,32},{48,56},{56,48},{64,72... | collective-permute-start | bytes 294920 | tf_op jit(solution)/shard_map/ppermute | solution.py:471
  7.2 0.9 %collective-permute-done = f32[96,256]{1,0:T(8,128)S(1)} collective-permute-done((f32[96,256]{1,0:T(8,128)S(1)}, f32[96,256]{1,0:T(8,128)S(1)}, u32[]{:S(2)}, u32[]{:S(2)}) %collective-permute-start) | collective-permute-done | bytes 98336 | tf_op jit(solution)/shard_map/ppermute | solution.py:471
  8.1 1.8 %collective-permute-start.1 = (f32[96,256]{1,0:T(8,128)S(1)}, f32[96,256]{1,0:T(8,128)S(1)}, u32[]{:S(2)}, u32[]{:S(2)}) collective-permute-start(f32[96,256]{1,0:T(8,128)S(1)} %add.17), channel_id=1, source_target_pairs={{0,16},{8,40},{16,0},{24,56},{32,48},{40,8},{48,32},{56,24},{64,80... | collective-permute-start | bytes 294920 | tf_op jit(solution)/shard_map/ppermute | solution.py:471
  9.9 2.3 %collective-permute-done.1 = f32[96,256]{1,0:T(8,128)S(1)} collective-permute-done((f32[96,256]{1,0:T(8,128)S(1)}, f32[96,256]{1,0:T(8,128)S(1)}, u32[]{:S(2)}, u32[]{:S(2)}) %collective-permute-start.1) | collective-permute-done | bytes 98336 | tf_op jit(solution)/shard_map/ppermute | solution.py:471
  12.3 1.4 %collective-permute-start.2 = (f32[96,256]{1,0:T(8,128)S(1)}, f32[96,256]{1,0:T(8,128)S(1)}, u32[]{:S(2)}, u32[]{:S(2)}) collective-permute-start(f32[96,256]{1,0:T(8,128)S(1)} %add.18), channel_id=1, source_target_pairs={{0,32},{8,24},{16,48},{24,8},{32,0},{40,56},{48,16},{56,40},{64,96... | collective-permute-start | bytes 294920 | tf_op jit(solution)/shard_map/ppermute | solution.py:471
  13.6 2.2 %collective-permute-done.2 = f32[96,256]{1,0:T(8,128)S(1)} collective-permute-done((f32[96,256]{1,0:T(8,128)S(1)}, f32[96,256]{1,0:T(8,128)S(1)}, u32[]{:S(2)}, u32[]{:S(2)}) %collective-permute-start.2) | collective-permute-done | bytes 98336 | tf_op jit(solution)/shard_map/ppermute | solution.py:471
  15.8 3.5 %collective-permute-start.3 = (f32[96,256]{1,0:T(8,128)S(1)}, f32[96,256]{1,0:T(8,128)S(1)}, u32[]{:S(2)}, u32[]{:S(2)}) collective-permute-start(f32[96,256]{1,0:T(8,128)S(1)} %add.19), channel_id=1, source_target_pairs={{0,64},{8,72},{16,80},{24,88},{32,96},{40,104},{48,112},{56,120},{... | collective-permute-start | bytes 294920 | tf_op jit(solution)/shard_map/ppermute | solution.py:471
  19.3 0.7 slice.3
  20.0 0.8 dynamic_slice.3
  20.8 1.0 %collective-permute-done.3 = f32[96,256]{1,0:T(8,128)S(1)} collective-permute-done((f32[96,256]{1,0:T(8,128)S(1)}, f32[96,256]{1,0:T(8,128)S(1)}, u32[]{:S(2)}, u32[]{:S(2)}) %collective-permute-start.3) | collective-permute-done | bytes 98336 | tf_op jit(solution)/shard_map/ppermute | solution.py:471
  21.8 2.8 %collective-permute-start.5 = (f32[1,96,256]{2,1,0:T(8,128)S(1)}, f32[1,96,256]{2,1,0:T(8,128)S(1)}, u32[]{:S(2)}, u32[]{:S(2)}) collective-permute-start(f32[1,96,256]{2,1,0:T(8,128)S(1)} %add_bitcast_fusion), channel_id=1, source_target_pairs={{0,8},{8,0},{16,24},{24,16},{32,40},{40,32},{48,56},{56,48},{64,72... | collective-permute-start | bytes 294920 | tf_op jit(solution)/shard_map/ppermute | solution.py:471
  24.6 2.9 %collective-permute-start.4 = (f32[1,96,256]{2,1,0:T(8,128)S(1)}, f32[1,96,256]{2,1,0:T(8,128)S(1)}, u32[]{:S(2)}, u32[]{:S(2)}) collective-permute-start(f32[1,96,256]{2,1,0:T(8,128)S(1)} %add_bitcast_fusion), channel_id=1, source_target_pairs={{0,4},{1,5},{2,6},{3,7},{4,0},{5,1},{6,2},{7,3},{8,12},{9,13},{10,... | collective-permute-start | bytes 294920 | tf_op jit(solution)/shard_map/ppermute | solution.py:471
  27.7 1.4 %picks.1 = (bf16[304,224]{1,0:T(8,128)(2,1)S(1)}, bf16[304,224]{1,0:T(8,128)(2,1)S(1)}, bf16[608,224]{1,0:T(8,128)(2,1)S(1)}, bf16[608,224]{1,0:T(8,128)(2,1)S(1)}) custom-call(s32[2]{0:T(128)S(1)} %pad_add_fusion.scal.refs_6_), custom_call_target="tpu_custom_call" | custom-call | tf_op jit(solution)/shard_map/picks/pallas_call | solution.py:74
  29.1 1.4 %collective-permute-done.4 = f32[1,96,256]{2,1,0:T(8,128)S(1)} collective-permute-done((f32[1,96,256]{2,1,0:T(8,128)S(1)}, f32[1,96,256]{2,1,0:T(8,128)S(1)}, u32[]{:S(2)}, u32[]{:S(2)}) %collective-permute-start.4) | collective-permute-done | bytes 98336 | tf_op jit(solution)/shard_map/ppermute | solution.py:471
  30.5 0.9 %collective-permute-start.7 = (f32[1,96,256]{2,1,0:T(8,128)S(1)}, f32[1,96,256]{2,1,0:T(8,128)S(1)}, u32[]{:S(2)}, u32[]{:S(2)}) collective-permute-start(f32[1,96,256]{2,1,0:T(8,128)S(1)} %collective-permute-done.4), channel_id=1, source_target_pairs={{0,8},{8,0},{16,24},{24,16},{32,40},{40,32},{48,56},{56,48},{64,72... | collective-permute-start | bytes 294920 | tf_op jit(solution)/shard_map/ppermute | solution.py:471
  31.4 2.8 %collective-permute-start.6 = (f32[2,96,256]{2,1,0:T(8,128)S(1)}, f32[2,96,256]{2,1,0:T(8,128)S(1)}, u32[]{:S(2)}, u32[]{:S(2)}) collective-permute-start(f32[2,96,256]{2,1,0:T(8,128)S(1)} %pad_maximum_fusion.1.refs_0_), channel_id=1, source_target_pairs={{0,2},{1,3},{2,0},{3,1},{4,6},{5,7},{6,4},{7,5},{8,10},{9,11},{10,... | collective-permute-start | bytes 589832 | tf_op jit(solution)/shard_map/ppermute | solution.py:471
  34.3 4.7 %early_first.1 = (f32[512,512]{1,0:T(8,128)S(1)}, f32[304,512]{1,0:T(8,128)S(1)}, f32[608,512]{1,0:T(8,128)S(1)}, f32[304,608]{1,0:T(8,128)S(1)}) custom-call(f32[2,96,256]{2,1,0:T(8,128)S(1)} %pad_maximum_fusion.1.refs_0_, f32[2,96,256]{2,1,0:T(8,128)S(1)} %constant_dynamic-update-slice_fusion.refs_1_.refs_6_, ...), custom_call_target="tpu_custom_call" | custom-call | flops 4000000000 | bytes 4194304 | tf_op jit(solution)/shard_map/early_first/pallas_call | solution.py:302
  39.5 0.8 collective-permute-start.9
  40.3 1.5 %collective-permute-start.8 = (f32[4,96,256]{2,1,0:T(8,128)S(1)}, f32[4,96,256]{2,1,0:T(8,128)S(1)}, u32[]{:S(2)}, u32[]{:S(2)}) collective-permute-start(f32[4,96,256]{2,1,0:T(8,128)S(1)} %pad_maximum_fusion), channel_id=1, source_target_pairs={{0,1},{1,0},{2,3},{3,2},{4,5},{5,4},{6,7},{7,6},{8,9},{9,8},{10,11... | collective-permute-start | bytes 1179656 | tf_op jit(solution)/shard_map/ppermute | solution.py:471
  41.8 11.2 %early_second.1 = (f32[512,512]{1,0:T(8,128)S(1)}, f32[304,512]{1,0:T(8,128)S(1)}, f32[304,512]{1,0:T(8,128)S(1)}, f32[608,512]{1,0:T(8,128)S(1)}, f32[304,608]{1,0:T(8,128)S(1)}) custom-call(f32[2,96,256]{2,1,0:T(8,128)S(1)} %collective-permute-done.6.refs_0_, f32[2,96,256]{2,1,0:T(8,128)S(1)} %collective-permute-done.9.refs_1_, ...), custom_call_target="tpu_custom_call" | custom-call | flops 4000000000 | bytes 4194304 | tf_op jit(solution)/shard_map/early_second/pallas_call | solution.py:302
  53.4 1.5 %late_corner.1 = (f32[2,512,512]{2,1,0:T(8,128)S(1)}, bf16[4,512,256]{2,1,0:T(8,128)(2,1)S(1)}, bf16[4,512,256]{2,1,0:T(8,128)(2,1)S(1)}) custom-call(f32[4,96,256]{2,1,0:T(8,128)S(1)} %collective-permute-done.8.c_ref.own), custom_call_target="tpu_custom_call" | custom-call | flops 1000000000 | bytes 4194304 | tf_op jit(solution)/shard_map/late_corner/pallas_call | solution.py:323
  54.9 26.5 %gram_factor.1 = (f32[297,594]{1,0:T(8,128)}, f32[297,512]{1,0:T(8,128)}) custom-call(s32[2]{0:T(128)S(1)} %pad_add_fusion.scal.refs_6_, f32[4,96,256]{2,1,0:T(8,128)S(1)} %collective-permute-done.8.c_ref.own, f32[4,96,256]{2,1,0:T(8,128)S(1)} %collective-permute-done.10.oth, bf16[304,224]{1,0:T(8,128)(2,1)S(1)} %get-tuple-element.51.refs_2_.lr, ...), custom_call_target="tpu_custom_call" | custom-call | tf_op jit(solution)/shard_map/gram_factor/pallas_call | solution.py:441
  (22 shorter events, 1.9 us)
Async XLA Ops:
  0.6 1.2 %copy-start = (bf16[96,4096]{1,0:T(8,128)(2,1)S(1)}, bf16[96,4096]{1,0:T(8,128)(2,1)}, u32[]{:S(2)}) copy-start(bf16[96,4096]{1,0:T(8,128)(2,1)} %param.5) | copy-start | bytes 2359300
  5.7 2.4 %collective-permute-start = (f32[96,256]{1,0:T(8,128)S(1)}, f32[96,256]{1,0:T(8,128)S(1)}, u32[]{:S(2)}, u32[]{:S(2)}) collective-permute-start(f32[96,256]{1,0:T(8,128)S(1)} %get-tuple-element.44), channel_id=1, source_target_pairs={{0,8},{8,0},{16,24},{24,16},{32,40},{40,32},{48,56},{56,48},{64,72... | collective-permute-start | bytes 294920 | tf_op jit(solution)/shard_map/ppermute | solution.py:471
  8.1 4.1 %collective-permute-start.1 = (f32[96,256]{1,0:T(8,128)S(1)}, f32[96,256]{1,0:T(8,128)S(1)}, u32[]{:S(2)}, u32[]{:S(2)}) collective-permute-start(f32[96,256]{1,0:T(8,128)S(1)} %add.17), channel_id=1, source_target_pairs={{0,16},{8,40},{16,0},{24,56},{32,48},{40,8},{48,32},{56,24},{64,80... | collective-permute-start | bytes 294920 | tf_op jit(solution)/shard_map/ppermute | solution.py:471
  12.3 3.5 %collective-permute-start.2 = (f32[96,256]{1,0:T(8,128)S(1)}, f32[96,256]{1,0:T(8,128)S(1)}, u32[]{:S(2)}, u32[]{:S(2)}) collective-permute-start(f32[96,256]{1,0:T(8,128)S(1)} %add.18), channel_id=1, source_target_pairs={{0,32},{8,24},{16,48},{24,8},{32,0},{40,56},{48,16},{56,40},{64,96... | collective-permute-start | bytes 294920 | tf_op jit(solution)/shard_map/ppermute | solution.py:471
  15.8 6.0 %collective-permute-start.3 = (f32[96,256]{1,0:T(8,128)S(1)}, f32[96,256]{1,0:T(8,128)S(1)}, u32[]{:S(2)}, u32[]{:S(2)}) collective-permute-start(f32[96,256]{1,0:T(8,128)S(1)} %add.19), channel_id=1, source_target_pairs={{0,64},{8,72},{16,80},{24,88},{32,96},{40,104},{48,112},{56,120},{... | collective-permute-start | bytes 294920 | tf_op jit(solution)/shard_map/ppermute | solution.py:471
  21.8 7.2 %collective-permute-start.5 = (f32[1,96,256]{2,1,0:T(8,128)S(1)}, f32[1,96,256]{2,1,0:T(8,128)S(1)}, u32[]{:S(2)}, u32[]{:S(2)}) collective-permute-start(f32[1,96,256]{2,1,0:T(8,128)S(1)} %add_bitcast_fusion), channel_id=1, source_target_pairs={{0,8},{8,0},{16,24},{24,16},{32,40},{40,32},{48,56},{56,48},{64,72... | collective-permute-start | bytes 294920 | tf_op jit(solution)/shard_map/ppermute | solution.py:471
  24.6 5.9 %collective-permute-start.4 = (f32[1,96,256]{2,1,0:T(8,128)S(1)}, f32[1,96,256]{2,1,0:T(8,128)S(1)}, u32[]{:S(2)}, u32[]{:S(2)}) collective-permute-start(f32[1,96,256]{2,1,0:T(8,128)S(1)} %add_bitcast_fusion), channel_id=1, source_target_pairs={{0,4},{1,5},{2,6},{3,7},{4,0},{5,1},{6,2},{7,3},{8,12},{9,13},{10,... | collective-permute-start | bytes 294920 | tf_op jit(solution)/shard_map/ppermute | solution.py:471
  30.5 3.7 %collective-permute-start.7 = (f32[1,96,256]{2,1,0:T(8,128)S(1)}, f32[1,96,256]{2,1,0:T(8,128)S(1)}, u32[]{:S(2)}, u32[]{:S(2)}) collective-permute-start(f32[1,96,256]{2,1,0:T(8,128)S(1)} %collective-permute-done.4), channel_id=1, source_target_pairs={{0,8},{8,0},{16,24},{24,16},{32,40},{40,32},{48,56},{56,48},{64,72... | collective-permute-start | bytes 294920 | tf_op jit(solution)/shard_map/ppermute | solution.py:471
  31.4 8.1 %collective-permute-start.6 = (f32[2,96,256]{2,1,0:T(8,128)S(1)}, f32[2,96,256]{2,1,0:T(8,128)S(1)}, u32[]{:S(2)}, u32[]{:S(2)}) collective-permute-start(f32[2,96,256]{2,1,0:T(8,128)S(1)} %pad_maximum_fusion.1.refs_0_), channel_id=1, source_target_pairs={{0,2},{1,3},{2,0},{3,1},{4,6},{5,7},{6,4},{7,5},{8,10},{9,11},{10,... | collective-permute-start | bytes 589832 | tf_op jit(solution)/shard_map/ppermute | solution.py:471
  39.5 2.3 %collective-permute-start.9 = (f32[2,96,256]{2,1,0:T(8,128)S(1)}, f32[2,96,256]{2,1,0:T(8,128)S(1)}, u32[]{:S(2)}, u32[]{:S(2)}) collective-permute-start(f32[2,96,256]{2,1,0:T(8,128)S(1)} %collective-permute-done.6.refs_0_), channel_id=1, source_target_pairs={{0,8},{8,0},{16,24},{24,16},{32,40},{40,32},{48,56},{56,48},{64,72... | collective-permute-start | bytes 589832 | tf_op jit(solution)/shard_map/ppermute | solution.py:471
  40.3 12.7 %collective-permute-start.8 = (f32[4,96,256]{2,1,0:T(8,128)S(1)}, f32[4,96,256]{2,1,0:T(8,128)S(1)}, u32[]{:S(2)}, u32[]{:S(2)}) collective-permute-start(f32[4,96,256]{2,1,0:T(8,128)S(1)} %pad_maximum_fusion), channel_id=1, source_target_pairs={{0,1},{1,0},{2,3},{3,2},{4,5},{5,4},{6,7},{7,6},{8,9},{9,8},{10,11... | collective-permute-start | bytes 1179656 | tf_op jit(solution)/shard_map/ppermute | solution.py:471
  53.0 1.9 %collective-permute-start.10 = (f32[4,96,256]{2,1,0:T(8,128)S(1)}, f32[4,96,256]{2,1,0:T(8,128)S(1)}, u32[]{:S(2)}, u32[]{:S(2)}) collective-permute-start(f32[4,96,256]{2,1,0:T(8,128)S(1)} %collective-permute-done.8.c_ref.own), channel_id=1, source_target_pairs={{0,8},{8,0},{16,24},{24,16},{32,40},{40,32},{48,56},{56,48},{64,72... | collective-permute-start | bytes 1179656 | tf_op jit(solution)/shard_map/ppermute | solution.py:471
where the time goes:
time: 81.6 us; the launch traced here: 81.4 us
  Pallas kernels  45.5 us (56%)
  starting transfers between devices  20.2 us (25%)
  waiting for transfers between devices  8.4 us (10%)
  matrix products  3.75 us (5%)
  local copies, waits for them, and re-layouts  2.62 us (3%)
    pallas_call x1, Pallas kernels, main(): pl.pallas_call(functools.partial(main_kernel, modes, scale), in_specs=[pl...  26.5 us
    ppermute x11, starting transfers between devices, swap(): lax.ppermute(value, axis, [(i, i ^ bits[i & 1]) for i in range(size)])  20.2 us
    pallas_call x2, Pallas kernels, early(): pl.pallas_call(functools.partial(early_kernel, modes, scale, first), in_s...  15.9 us
    ppermute x11, waiting for transfers between devices, swap(): lax.ppermute(value, axis, [(i, i ^ bits[i & 1]) for i in range(size)])  8.4 us
    dot_general x1, matrix products, per_device(): lax.dot_general(snapshots, pod_basis, NT, preferred_element_type=F32)  3.44 us
  transfers between devices with their start and end apart: 11, of which 6 were waited for; matrix products, arithmetic and copies ran while one was open for 2% of the time, Pallas kernels for 23%

commit v1 on v0

--- a/solution.py
+++ b/solution.py
@@ -96,12 +96,18 @@
         fh[t + i], fl[t + i] = split(f_s[i])
 
 
+def corner_part(t, fh, fl, at):
+    def one(i):
+        h, l = fh[t + i], fl[t + i]
+        rows = slice(at, at + HALF)
+        return dot3((h[rows], l[rows]), (h[at:], l[at:]))
+
+    return one(0) + one(1)
+
+
 def corner_pair(t, fh, fl, a_ref):
-    pairs = [(fh[t + i], fl[t + i]) for i in range(2)]
-    top = [dot3((h[0:HALF], l[0:HALF]), (h, l)) for h, l in pairs]
-    low = [dot3((h[HALF:], l[HALF:]), (h[HALF:], l[HALF:])) for h, l in pairs]
-    a_ref[0:HALF, :] = top[0] + top[1]
-    a_ref[HALF:, HALF:] = low[0] + low[1]
+    a_ref[0:HALF, :] = corner_part(t, fh, fl, 0)
+    a_ref[HALF:, HALF:] = corner_part(t, fh, fl, HALF)
 
 
 def lane_bcast(x, c):
@@ -132,22 +138,22 @@
     strips = STEP // 8
     sub = lax.broadcasted_iota(jnp.int32, (8, 128), 0)
     T = [[s_ref[lo + 8 * r : lo + 8 * r + 8, 0:128], s_ref[lo + 8 * r : lo + 8 * r + 8, 128:256]] for r in range(strips)]
-    B = {(r, j): lane_bcast(T[r][0], lo + j) for j in range(STEP) for r in range(j // 8, strips)}
     for q in range(strips):
+        cols = range(8 * q, 8 * q + 8)
+        B = {(r, j): lane_bcast(T[r][0], lo + j) for j in cols for r in range(q, strips)}
         scale = None
-        for k in range(8 * q, 8 * q + 8):
+        for k in cols:
             rs = lax.rsqrt(sub_bcast(B[q, k], k - 8 * q))
             inv = rs * rs
             scale = rs if scale is None else jnp.where(sub == k - 8 * q, rs, scale)
             row = [sub_bcast(part, k - 8 * q) for part in T[q]]
-            pivots = {j: sub_bcast(B[j // 8, k], j % 8) for j in range(k + 1, STEP)}
+            pivots = {j: sub_bcast(B[q, k], j - 8 * q) for j in range(k + 1, 8 * q + 8)}
             for r in range(q, strips):
                 m = B[r, k] * inv
                 if r == q:
                     m = jnp.where(sub > k - 8 * q, m, 0.0)
-                for j in range(k + 1, STEP):
-                    if j // 8 <= r:
-                        B[r, j] = B[r, j] - m * pivots[j]
+                for j in pivots:
+                    B[r, j] = B[r, j] - m * pivots[j]
                 T[r] = [part - m * line for part, line in zip(T[r], row)]
         T[q] = [part * scale for part in T[q]]
         between(4 * b + q)
@@ -208,13 +214,15 @@
     def part1():
         gr[...] += dot3(env["fr"], env["fp"])
 
-    def part2():
-        gc[...] += dot3(env["fc"], env["fp"])
+    def part2(at):
+        gc[at, :] += dot3(tuple(half[at] for half in env["fc"]), env["fp"])
 
     def part3():
         gt[...] += dot3(env["fr"], env["fc"])
 
-    return [part0, part1, part2, part3]
+    mid = gc.shape[0] // 2
+    lower, upper = slice(0, mid), slice(mid, 2 * mid)
+    return [part0, part1, lambda: part2(lower), part3, lambda: part2(upper)]
 
 
 def pair_inverse(p, inv_s, low_s):
@@ -262,23 +270,24 @@
         return carry
 
     if first:
+        lax.fori_loop(0, 2, corner_body, 0)
+    else:
         corner_body(0, 0)
         corner_body(1, 0)
-    else:
-        lax.fori_loop(0, 2, corner_body, 0)
     a_out[...] = a_s[0] + a_s[1]
 
-    def pair_body(i, carry):
-        for t in (2 * i, 2 * i + 1):
-            for part in block_parts(t, c_s, fh, fl, lr, rr, lc, rc, pair_s.at[i], gc, gt, modes):
+    def gram_body(i, carry):
+        together = 1 if first else 3
+        for t in range(together):
+            t = together * i + t
+            for part in block_parts(t, c_s, fh, fl, lr, rr, lc, rc, pair_s.at[t // 2], gc, gt, modes):
                 part()
         return carry
 
+    lax.fori_loop(0, 2, gram_body, 0)
     if first:
-        pair_body(0, 0)
         gr[...] = pair_s[0]
     else:
-        lax.fori_loop(0, 3, pair_body, 0)
         gr[...] = gr_in[...] + pair_s[0]
         gr_oth[...] = pair_s[2] + pair_s[1]
 
@@ -370,12 +379,21 @@
 
     def corner_body(i, carry):
         panel_pair(2 * i, oth, f_s, fh, fl, modes, scale)
-        corner_pair(2 * i, fh, fl, a_p.at[i])
+        a_p[i] = corner_part(2 * i, fh, fl, 0)
         return carry
 
     lax.fori_loop(0, 2, corner_body, 0)
-    total = (a0[...] + a1[...]) + ((a_own[0] + a_p[0]) + (a_own[1] + a_p[1]))
-    a_s[...] = total + diagonal(a_s.shape, 0, 0, ridge_panel[...])
+    a_s[...] = diagonal(a_s.shape, 0, 0, ridge_panel[...])
+
+    def add_corner(rows, cols, late):
+        early_sum = a0[rows, cols] + a1[rows, cols]
+        a_s[rows, cols] += early_sum + ((a_own[0, rows, cols] + late[0]) + (a_own[1, rows, cols] + late[1]))
+
+    def add_low():
+        half = slice(HALF, PANEL)
+        add_corner(half, half, [corner_part(2 * i, fh, fl, HALF) for i in range(2)])
+
+    add_corner(slice(0, HALF), slice(0, PANEL), a_p)
     gr[...] = jnp.zeros_like(gr)
     gc[...] = gc_in[...]
     gt[...] = gt_in[...]
@@ -385,15 +403,20 @@
         held = (own, own_h, own_l) if t < 4 else (oth, fh, fl)
         parts += block_parts(t % 4, *held, lr, rr, lc, rc, gr.at[t // 2], gc, gt, modes)
 
-    def solve_first():
-        inverse = pair_inverse(0, inv_s, low_s)
-        cross = u_s[0:HALF, HALF:]
+    def solve_first(p, at, g):
+        first = dot(g[:, 0:HALF], pair_inverse(0, inv_s, low_s), NT, HI)
+        p[at, 0:HALF] = first
+        p[at, HALF:] = g[:, HALF:] - dot(first, u_s[0:HALF, HALF:], NN, HI)
+
+    def solve_rows():
         line = diagonal(pr.shape, first_row, 0, ridge_panel[...])
         sums = (gr_in[...] + (gr[0] + gr[1])) + (gr_oth_in[...] + (gr[2] + gr[3])) + line
-        for p, g in ((pr, sums), (pc, gc[...])):
-            first = dot(g[:, 0:HALF], inverse, NT, HI)
-            p[:, 0:HALF] = first
-            p[:, HALF:] = g[:, HALF:] - dot(first, cross, NN, HI)
+        solve_first(pr, slice(0, pr.shape[0]), sums)
+
+    def solve_cols(i):
+        mid = pc.shape[0] // 2
+        at = slice(mid * i, mid * i + mid)
+        solve_first(pc, at, gc[at, :])
 
     def update(at):
         ri = first_row + lax.broadcasted_iota(jnp.int32, gt.shape, 0)
@@ -412,9 +435,12 @@
 
     slots = [[] for _ in range(64)]
     for i, part in enumerate(parts):
-        slots[i * 48 // len(parts)].append(part)
-    slots[49].append(solve_first)
-    slots[54].append(update_first)
+        slots[i * 50 // len(parts)].append(part)
+    slots[20].append(add_low)
+    slots[51].append(solve_rows)
+    slots[53].append(lambda: solve_cols(0))
+    slots[55].append(lambda: solve_cols(1))
+    slots[58].append(update_first)
 
     def between_of(k):
         def between(i):
@@ -447,7 +473,7 @@
             pltpu.VMEM((2, PANEL, n), F32),
             pltpu.VMEM((4, PANEL, n), BF16),
             pltpu.VMEM((4, PANEL, n), BF16),
-            pltpu.VMEM((2, PANEL, PANEL), F32),
+            pltpu.VMEM((2, HALF, PANEL), F32),
             pltpu.VMEM((PANEL, PANEL), F32),
             pltpu.VMEM((BLOCK, 2 * BLOCK), F32),
             pltpu.VMEM((BLOCK, BLOCK), F32),

time: 81.6 us -> 80 us (0.980)
    pallas_call x1, Pallas kernels: 26.5 us -> 25.5 us  [main(): pl.pallas_call(functools.partial(main_kernel, modes, scale), in_specs=[pl...]
  transfers between devices with their start and end apart: 11 -> 11, of which waited for: 6 -> 5; matrix products, arithmetic and copies ran while one was open for 2% -> 2% of each run, Pallas kernels for 23% -> 24%
where the time goes in v1:
time: 80 us; the launch traced here: 79.7 us
  Pallas kernels  44.7 us (56%)
  starting transfers between devices  19.8 us (25%)
  waiting for transfers between devices  7.89 us (10%)
  matrix products  3.75 us (5%)
  local copies, waits for them, and re-layouts  2.62 us (3%)
    pallas_call x1, Pallas kernels, main(): pl.pallas_call(functools.partial(main_kernel, modes, scale), in_specs=[pl...  25.5 us
    ppermute x11, starting transfers between devices, swap(): lax.ppermute(value, axis, [(i, i ^ bits[i & 1]) for i in range(size)])  19.8 us
    pallas_call x2, Pallas kernels, early(): pl.pallas_call(functools.partial(early_kernel, modes, scale, first), in_s...  16.1 us
    ppermute x11, waiting for transfers between devices, swap(): lax.ppermute(value, axis, [(i, i ^ bits[i & 1]) for i in range(size)])  7.89 us
    dot_general x1, matrix products, per_device(): lax.dot_general(snapshots, pod_basis, NT, preferred_element_type=F32)  3.44 us
  transfers between devices with their start and end apart: 11, of which 5 were waited for; matrix products, arithmetic and copies ran while one was open for 2% of the time, Pallas kernels for 24%

profile of v1, /device:TPU:1, one launch (start us, length us, event | category | flops | bytes accessed | tf_op | source)
XLA Modules:
  0.0 79.7 jit_solution(15121249065006461551)
XLA Ops:
  0.7 0.8 reshape.7
  2.1 3.4 %fusion.part = f32[512,96]{1,0:T(8,128)S(1)} fusion(bf16[512,4096]{1,0:T(8,128)(2,1)} %param.4, bf16[96,4096]{1,0:T(8,128)(2,1)S(1)} %copy-done), kind=kOutput, calls=%fused_computation.6 | convolution fusion | flops 402653184 | bytes 5177344 | tf_op jit(solution)/shard_map/dot_general | solution.py:521
  5.7 1.5 %collective-permute-start = (f32[96,256]{1,0:T(8,128)S(1)}, f32[96,256]{1,0:T(8,128)S(1)}, u32[]{:S(2)}, u32[]{:S(2)}) collective-permute-start(f32[96,256]{1,0:T(8,128)S(1)} %get-tuple-element.44), channel_id=1, source_target_pairs={{0,8},{8,0},{16,24},{24,16},{32,40},{40,32},{48,56},{56,48},{64,72... | collective-permute-start | bytes 294920 | tf_op jit(solution)/shard_map/ppermute | solution.py:497
  7.2 0.9 %collective-permute-done = f32[96,256]{1,0:T(8,128)S(1)} collective-permute-done((f32[96,256]{1,0:T(8,128)S(1)}, f32[96,256]{1,0:T(8,128)S(1)}, u32[]{:S(2)}, u32[]{:S(2)}) %collective-permute-start) | collective-permute-done | bytes 98336 | tf_op jit(solution)/shard_map/ppermute | solution.py:497
  8.1 1.8 %collective-permute-start.1 = (f32[96,256]{1,0:T(8,128)S(1)}, f32[96,256]{1,0:T(8,128)S(1)}, u32[]{:S(2)}, u32[]{:S(2)}) collective-permute-start(f32[96,256]{1,0:T(8,128)S(1)} %add.17), channel_id=1, source_target_pairs={{0,16},{8,40},{16,0},{24,56},{32,48},{40,8},{48,32},{56,24},{64,80... | collective-permute-start | bytes 294920 | tf_op jit(solution)/shard_map/ppermute | solution.py:497
  9.9 2.3 %collective-permute-done.1 = f32[96,256]{1,0:T(8,128)S(1)} collective-permute-done((f32[96,256]{1,0:T(8,128)S(1)}, f32[96,256]{1,0:T(8,128)S(1)}, u32[]{:S(2)}, u32[]{:S(2)}) %collective-permute-start.1) | collective-permute-done | bytes 98336 | tf_op jit(solution)/shard_map/ppermute | solution.py:497
  12.3 1.4 %collective-permute-start.2 = (f32[96,256]{1,0:T(8,128)S(1)}, f32[96,256]{1,0:T(8,128)S(1)}, u32[]{:S(2)}, u32[]{:S(2)}) collective-permute-start(f32[96,256]{1,0:T(8,128)S(1)} %add.18), channel_id=1, source_target_pairs={{0,32},{8,24},{16,48},{24,8},{32,0},{40,56},{48,16},{56,40},{64,96... | collective-permute-start | bytes 294920 | tf_op jit(solution)/shard_map/ppermute | solution.py:497
  13.6 2.2 %collective-permute-done.2 = f32[96,256]{1,0:T(8,128)S(1)} collective-permute-done((f32[96,256]{1,0:T(8,128)S(1)}, f32[96,256]{1,0:T(8,128)S(1)}, u32[]{:S(2)}, u32[]{:S(2)}) %collective-permute-start.2) | collective-permute-done | bytes 98336 | tf_op jit(solution)/shard_map/ppermute | solution.py:497
  15.8 3.5 %collective-permute-start.3 = (f32[96,256]{1,0:T(8,128)S(1)}, f32[96,256]{1,0:T(8,128)S(1)}, u32[]{:S(2)}, u32[]{:S(2)}) collective-permute-start(f32[96,256]{1,0:T(8,128)S(1)} %add.19), channel_id=1, source_target_pairs={{0,64},{8,72},{16,80},{24,88},{32,96},{40,104},{48,112},{56,120},{... | collective-permute-start | bytes 294920 | tf_op jit(solution)/shard_map/ppermute | solution.py:497
  19.3 0.7 slice.3
  20.0 0.8 dynamic_slice.3
  20.8 1.0 %collective-permute-done.3 = f32[96,256]{1,0:T(8,128)S(1)} collective-permute-done((f32[96,256]{1,0:T(8,128)S(1)}, f32[96,256]{1,0:T(8,128)S(1)}, u32[]{:S(2)}, u32[]{:S(2)}) %collective-permute-start.3) | collective-permute-done | bytes 98336 | tf_op jit(solution)/shard_map/ppermute | solution.py:497
  21.8 2.8 %collective-permute-start.5 = (f32[1,96,256]{2,1,0:T(8,128)S(1)}, f32[1,96,256]{2,1,0:T(8,128)S(1)}, u32[]{:S(2)}, u32[]{:S(2)}) collective-permute-start(f32[1,96,256]{2,1,0:T(8,128)S(1)} %add_bitcast_fusion), channel_id=1, source_target_pairs={{0,8},{8,0},{16,24},{24,16},{32,40},{40,32},{48,56},{56,48},{64,72... | collective-permute-start | bytes 294920 | tf_op jit(solution)/shard_map/ppermute | solution.py:497
  24.6 2.9 %collective-permute-start.4 = (f32[1,96,256]{2,1,0:T(8,128)S(1)}, f32[1,96,256]{2,1,0:T(8,128)S(1)}, u32[]{:S(2)}, u32[]{:S(2)}) collective-permute-start(f32[1,96,256]{2,1,0:T(8,128)S(1)} %add_bitcast_fusion), channel_id=1, source_target_pairs={{0,4},{1,5},{2,6},{3,7},{4,0},{5,1},{6,2},{7,3},{8,12},{9,13},{10,... | collective-permute-start | bytes 294920 | tf_op jit(solution)/shard_map/ppermute | solution.py:497
  27.7 1.4 %picks.1 = (bf16[304,224]{1,0:T(8,128)(2,1)S(1)}, bf16[304,224]{1,0:T(8,128)(2,1)S(1)}, bf16[608,224]{1,0:T(8,128)(2,1)S(1)}, bf16[608,224]{1,0:T(8,128)(2,1)S(1)}) custom-call(s32[2]{0:T(128)S(1)} %pad_add_fusion.scal.refs_6_), custom_call_target="tpu_custom_call" | custom-call | tf_op jit(solution)/shard_map/picks/pallas_call | solution.py:74
  29.1 1.4 %collective-permute-done.4 = f32[1,96,256]{2,1,0:T(8,128)S(1)} collective-permute-done((f32[1,96,256]{2,1,0:T(8,128)S(1)}, f32[1,96,256]{2,1,0:T(8,128)S(1)}, u32[]{:S(2)}, u32[]{:S(2)}) %collective-permute-start.4) | collective-permute-done | bytes 98336 | tf_op jit(solution)/shard_map/ppermute | solution.py:497
  30.5 0.9 %collective-permute-start.7 = (f32[1,96,256]{2,1,0:T(8,128)S(1)}, f32[1,96,256]{2,1,0:T(8,128)S(1)}, u32[]{:S(2)}, u32[]{:S(2)}) collective-permute-start(f32[1,96,256]{2,1,0:T(8,128)S(1)} %collective-permute-done.4), channel_id=1, source_target_pairs={{0,8},{8,0},{16,24},{24,16},{32,40},{40,32},{48,56},{56,48},{64,72... | collective-permute-start | bytes 294920 | tf_op jit(solution)/shard_map/ppermute | solution.py:497
  31.4 2.8 %collective-permute-start.6 = (f32[2,96,256]{2,1,0:T(8,128)S(1)}, f32[2,96,256]{2,1,0:T(8,128)S(1)}, u32[]{:S(2)}, u32[]{:S(2)}) collective-permute-start(f32[2,96,256]{2,1,0:T(8,128)S(1)} %pad_maximum_fusion.1.refs_0_), channel_id=1, source_target_pairs={{0,2},{1,3},{2,0},{3,1},{4,6},{5,7},{6,4},{7,5},{8,10},{9,11},{10,... | collective-permute-start | bytes 589832 | tf_op jit(solution)/shard_map/ppermute | solution.py:497
  34.3 5.7 %early_first.1 = (f32[512,512]{1,0:T(8,128)S(1)}, f32[304,512]{1,0:T(8,128)S(1)}, f32[608,512]{1,0:T(8,128)S(1)}, f32[304,608]{1,0:T(8,128)S(1)}) custom-call(f32[2,96,256]{2,1,0:T(8,128)S(1)} %pad_maximum_fusion.1.refs_0_, f32[2,96,256]{2,1,0:T(8,128)S(1)} %constant_dynamic-update-slice_fusion.refs_1_.refs_6_, ...), custom_call_target="tpu_custom_call" | custom-call | flops 4000000000 | bytes 4194304 | tf_op jit(solution)/shard_map/early_first/pallas_call | solution.py:311
  40.3 1.5 %collective-permute-start.8 = (f32[4,96,256]{2,1,0:T(8,128)S(1)}, f32[4,96,256]{2,1,0:T(8,128)S(1)}, u32[]{:S(2)}, u32[]{:S(2)}) collective-permute-start(f32[4,96,256]{2,1,0:T(8,128)S(1)} %pad_maximum_fusion), channel_id=1, source_target_pairs={{0,1},{1,0},{2,3},{3,2},{4,5},{5,4},{6,7},{7,6},{8,9},{9,8},{10,11... | collective-permute-start | bytes 1179656 | tf_op jit(solution)/shard_map/ppermute | solution.py:497
  41.8 10.5 %early_second.1 = (f32[512,512]{1,0:T(8,128)S(1)}, f32[304,512]{1,0:T(8,128)S(1)}, f32[304,512]{1,0:T(8,128)S(1)}, f32[608,512]{1,0:T(8,128)S(1)}, f32[304,608]{1,0:T(8,128)S(1)}) custom-call(f32[2,96,256]{2,1,0:T(8,128)S(1)} %collective-permute-done.6.refs_0_, f32[2,96,256]{2,1,0:T(8,128)S(1)} %collective-permute-done.9.refs_1_, ...), custom_call_target="tpu_custom_call" | custom-call | flops 4000000000 | bytes 4194304 | tf_op jit(solution)/shard_map/early_second/pallas_call | solution.py:311
  52.3 0.4 collective-permute-start.10
  52.7 1.6 %late_corner.1 = (f32[2,512,512]{2,1,0:T(8,128)S(1)}, bf16[4,512,256]{2,1,0:T(8,128)(2,1)S(1)}, bf16[4,512,256]{2,1,0:T(8,128)(2,1)S(1)}) custom-call(f32[4,96,256]{2,1,0:T(8,128)S(1)} %collective-permute-done.8.c_ref.own), custom_call_target="tpu_custom_call" | custom-call | flops 1000000000 | bytes 4194304 | tf_op jit(solution)/shard_map/late_corner/pallas_call | solution.py:332
  54.3 25.5 %gram_factor.1 = (f32[297,594]{1,0:T(8,128)}, f32[297,512]{1,0:T(8,128)}) custom-call(s32[2]{0:T(128)S(1)} %pad_add_fusion.scal.refs_6_, f32[4,96,256]{2,1,0:T(8,128)S(1)} %collective-permute-done.8.c_ref.own, f32[4,96,256]{2,1,0:T(8,128)S(1)} %collective-permute-done.10.oth, bf16[304,224]{1,0:T(8,128)(2,1)S(1)} %get-tuple-element.51.refs_2_.lr, ...), custom_call_target="tpu_custom_call" | custom-call | tf_op jit(solution)/shard_map/gram_factor/pallas_call | solution.py:467
  (22 shorter events, 1.4 us)
Async XLA Ops:
  0.6 1.2 %copy-start = (bf16[96,4096]{1,0:T(8,128)(2,1)S(1)}, bf16[96,4096]{1,0:T(8,128)(2,1)}, u32[]{:S(2)}) copy-start(bf16[96,4096]{1,0:T(8,128)(2,1)} %param.5) | copy-start | bytes 2359300
  5.7 2.4 %collective-permute-start = (f32[96,256]{1,0:T(8,128)S(1)}, f32[96,256]{1,0:T(8,128)S(1)}, u32[]{:S(2)}, u32[]{:S(2)}) collective-permute-start(f32[96,256]{1,0:T(8,128)S(1)} %get-tuple-element.44), channel_id=1, source_target_pairs={{0,8},{8,0},{16,24},{24,16},{32,40},{40,32},{48,56},{56,48},{64,72... | collective-permute-start | bytes 294920 | tf_op jit(solution)/shard_map/ppermute | solution.py:497
  8.1 4.1 %collective-permute-start.1 = (f32[96,256]{1,0:T(8,128)S(1)}, f32[96,256]{1,0:T(8,128)S(1)}, u32[]{:S(2)}, u32[]{:S(2)}) collective-permute-start(f32[96,256]{1,0:T(8,128)S(1)} %add.17), channel_id=1, source_target_pairs={{0,16},{8,40},{16,0},{24,56},{32,48},{40,8},{48,32},{56,24},{64,80... | collective-permute-start | bytes 294920 | tf_op jit(solution)/shard_map/ppermute | solution.py:497
  12.3 3.5 %collective-permute-start.2 = (f32[96,256]{1,0:T(8,128)S(1)}, f32[96,256]{1,0:T(8,128)S(1)}, u32[]{:S(2)}, u32[]{:S(2)}) collective-permute-start(f32[96,256]{1,0:T(8,128)S(1)} %add.18), channel_id=1, source_target_pairs={{0,32},{8,24},{16,48},{24,8},{32,0},{40,56},{48,16},{56,40},{64,96... | collective-permute-start | bytes 294920 | tf_op jit(solution)/shard_map/ppermute | solution.py:497
  15.8 6.0 %collective-permute-start.3 = (f32[96,256]{1,0:T(8,128)S(1)}, f32[96,256]{1,0:T(8,128)S(1)}, u32[]{:S(2)}, u32[]{:S(2)}) collective-permute-start(f32[96,256]{1,0:T(8,128)S(1)} %add.19), channel_id=1, source_target_pairs={{0,64},{8,72},{16,80},{24,88},{32,96},{40,104},{48,112},{56,120},{... | collective-permute-start | bytes 294920 | tf_op jit(solution)/shard_map/ppermute | solution.py:497
  21.8 7.2 %collective-permute-start.5 = (f32[1,96,256]{2,1,0:T(8,128)S(1)}, f32[1,96,256]{2,1,0:T(8,128)S(1)}, u32[]{:S(2)}, u32[]{:S(2)}) collective-permute-start(f32[1,96,256]{2,1,0:T(8,128)S(1)} %add_bitcast_fusion), channel_id=1, source_target_pairs={{0,8},{8,0},{16,24},{24,16},{32,40},{40,32},{48,56},{56,48},{64,72... | collective-permute-start | bytes 294920 | tf_op jit(solution)/shard_map/ppermute | solution.py:497
  24.6 5.9 %collective-permute-start.4 = (f32[1,96,256]{2,1,0:T(8,128)S(1)}, f32[1,96,256]{2,1,0:T(8,128)S(1)}, u32[]{:S(2)}, u32[]{:S(2)}) collective-permute-start(f32[1,96,256]{2,1,0:T(8,128)S(1)} %add_bitcast_fusion), channel_id=1, source_target_pairs={{0,4},{1,5},{2,6},{3,7},{4,0},{5,1},{6,2},{7,3},{8,12},{9,13},{10,... | collective-permute-start | bytes 294920 | tf_op jit(solution)/shard_map/ppermute | solution.py:497
  30.5 3.7 %collective-permute-start.7 = (f32[1,96,256]{2,1,0:T(8,128)S(1)}, f32[1,96,256]{2,1,0:T(8,128)S(1)}, u32[]{:S(2)}, u32[]{:S(2)}) collective-permute-start(f32[1,96,256]{2,1,0:T(8,128)S(1)} %collective-permute-done.4), channel_id=1, source_target_pairs={{0,8},{8,0},{16,24},{24,16},{32,40},{40,32},{48,56},{56,48},{64,72... | collective-permute-start | bytes 294920 | tf_op jit(solution)/shard_map/ppermute | solution.py:497
  31.4 8.5 %collective-permute-start.6 = (f32[2,96,256]{2,1,0:T(8,128)S(1)}, f32[2,96,256]{2,1,0:T(8,128)S(1)}, u32[]{:S(2)}, u32[]{:S(2)}) collective-permute-start(f32[2,96,256]{2,1,0:T(8,128)S(1)} %pad_maximum_fusion.1.refs_0_), channel_id=1, source_target_pairs={{0,2},{1,3},{2,0},{3,1},{4,6},{5,7},{6,4},{7,5},{8,10},{9,11},{10,... | collective-permute-start | bytes 589832 | tf_op jit(solution)/shard_map/ppermute | solution.py:497
  39.9 1.9 %collective-permute-start.9 = (f32[2,96,256]{2,1,0:T(8,128)S(1)}, f32[2,96,256]{2,1,0:T(8,128)S(1)}, u32[]{:S(2)}, u32[]{:S(2)}) collective-permute-start(f32[2,96,256]{2,1,0:T(8,128)S(1)} %collective-permute-done.6.refs_0_), channel_id=1, source_target_pairs={{0,8},{8,0},{16,24},{24,16},{32,40},{40,32},{48,56},{56,48},{64,72... | collective-permute-start | bytes 589832 | tf_op jit(solution)/shard_map/ppermute | solution.py:497
  40.3 12.0 %collective-permute-start.8 = (f32[4,96,256]{2,1,0:T(8,128)S(1)}, f32[4,96,256]{2,1,0:T(8,128)S(1)}, u32[]{:S(2)}, u32[]{:S(2)}) collective-permute-start(f32[4,96,256]{2,1,0:T(8,128)S(1)} %pad_maximum_fusion), channel_id=1, source_target_pairs={{0,1},{1,0},{2,3},{3,2},{4,5},{5,4},{6,7},{7,6},{8,9},{9,8},{10,11... | collective-permute-start | bytes 1179656 | tf_op jit(solution)/shard_map/ppermute | solution.py:497
  52.3 1.9 %collective-permute-start.10 = (f32[4,96,256]{2,1,0:T(8,128)S(1)}, f32[4,96,256]{2,1,0:T(8,128)S(1)}, u32[]{:S(2)}, u32[]{:S(2)}) collective-permute-start(f32[4,96,256]{2,1,0:T(8,128)S(1)} %collective-permute-done.8.c_ref.own), channel_id=1, source_target_pairs={{0,8},{8,0},{16,24},{24,16},{32,40},{40,32},{48,56},{56,48},{64,72... | collective-permute-start | bytes 1179656 | tf_op jit(solution)/shard_map/ppermute | solution.py:497

commit v2 on v1

--- a/solution.py
+++ b/solution.py
@@ -202,8 +202,9 @@
     return split(dot(left, cs, NN) * dot(right, cs, NN))
 
 
-def block_parts(t, c_s, fh, fl, lr, rr, lc, rc, gr, gc, gt, modes):
+def block_parts(t, c_s, fh, fl, lr, rr, lc, rc, gr, gc, gt, modes, start=None):
     env = {}
+    gr_was, gc_was, gt_was = start or (gr, gc, gt)
 
     def part0():
         cs = stacked(c_s[t], modes)
@@ -212,13 +213,14 @@
         env["fp"] = (fh[t], fl[t])
 
     def part1():
-        gr[...] += dot3(env["fr"], env["fp"])
+        value = dot3(env["fr"], env["fp"])
+        gr[...] = value if gr_was is None else gr_was[...] + value
 
     def part2(at):
-        gc[at, :] += dot3(tuple(half[at] for half in env["fc"]), env["fp"])
+        gc[at, :] = gc_was[at, :] + dot3(tuple(half[at] for half in env["fc"]), env["fp"])
 
     def part3():
-        gt[...] += dot3(env["fr"], env["fc"])
+        gt[...] = gt_was[...] + dot3(env["fr"], env["fc"])
 
     mid = gc.shape[0] // 2
     lower, upper = slice(0, mid), slice(mid, 2 * mid)
@@ -394,14 +396,13 @@
         add_corner(half, half, [corner_part(2 * i, fh, fl, HALF) for i in range(2)])
 
     add_corner(slice(0, HALF), slice(0, PANEL), a_p)
-    gr[...] = jnp.zeros_like(gr)
-    gc[...] = gc_in[...]
-    gt[...] = gt_in[...]
 
     parts = []
     for t in range(LATE):
         held = (own, own_h, own_l) if t < 4 else (oth, fh, fl)
-        parts += block_parts(t % 4, *held, lr, rr, lc, rc, gr.at[t // 2], gc, gt, modes)
+        pair = gr.at[t // 2]
+        start = (pair if t % 2 else None, gc if t else gc_in, gt if t else gt_in)
+        parts += block_parts(t % 4, *held, lr, rr, lc, rc, pair, gc, gt, modes, start)
 
     def solve_first(p, at, g):
         first = dot(g[:, 0:HALF], pair_inverse(0, inv_s, low_s), NT, HI)

time: 80 us -> 80 us (level)
  no operation moved by 1% of the time
where the time goes in v2:
time: 80 us; the launch traced here: 79.7 us
  Pallas kernels  44.7 us (56%)
  starting transfers between devices  19.8 us (25%)
  waiting for transfers between devices  7.89 us (10%)
  matrix products  3.75 us (5%)
  local copies, waits for them, and re-layouts  2.62 us (3%)
    pallas_call x1, Pallas kernels, main(): pl.pallas_call(functools.partial(main_kernel, modes, scale), in_specs=[pl...  25.4 us
    ppermute x11, starting transfers between devices, swap(): lax.ppermute(value, axis, [(i, i ^ bits[i & 1]) for i in range(size)])  19.8 us
    pallas_call x2, Pallas kernels, early(): pl.pallas_call(functools.partial(early_kernel, modes, scale, first), in_s...  16.1 us
    ppermute x11, waiting for transfers between devices, swap(): lax.ppermute(value, axis, [(i, i ^ bits[i & 1]) for i in range(size)])  7.89 us
    dot_general x1, matrix products, per_device(): lax.dot_general(snapshots, pod_basis, NT, preferred_element_type=F32)  3.44 us
  transfers between devices with their start and end apart: 11, of which 5 were waited for; matrix products, arithmetic and copies ran while one was open for 2% of the time, Pallas kernels for 24%

profile of v2, /device:TPU:1, one launch (start us, length us, event | category | flops | bytes accessed | tf_op | source)
XLA Modules:
  0.0 79.7 jit_solution(10953270779763778772)
XLA Ops:
  0.7 0.8 reshape.7
  2.1 3.4 %fusion.part = f32[512,96]{1,0:T(8,128)S(1)} fusion(bf16[512,4096]{1,0:T(8,128)(2,1)} %param.4, bf16[96,4096]{1,0:T(8,128)(2,1)S(1)} %copy-done), kind=kOutput, calls=%fused_computation.6 | convolution fusion | flops 402653184 | bytes 5177344 | tf_op jit(solution)/shard_map/dot_general | solution.py:522
  5.7 1.5 %collective-permute-start = (f32[96,256]{1,0:T(8,128)S(1)}, f32[96,256]{1,0:T(8,128)S(1)}, u32[]{:S(2)}, u32[]{:S(2)}) collective-permute-start(f32[96,256]{1,0:T(8,128)S(1)} %get-tuple-element.44), channel_id=1, source_target_pairs={{0,8},{8,0},{16,24},{24,16},{32,40},{40,32},{48,56},{56,48},{64,72... | collective-permute-start | bytes 294920 | tf_op jit(solution)/shard_map/ppermute | solution.py:498
  7.2 0.9 %collective-permute-done = f32[96,256]{1,0:T(8,128)S(1)} collective-permute-done((f32[96,256]{1,0:T(8,128)S(1)}, f32[96,256]{1,0:T(8,128)S(1)}, u32[]{:S(2)}, u32[]{:S(2)}) %collective-permute-start) | collective-permute-done | bytes 98336 | tf_op jit(solution)/shard_map/ppermute | solution.py:498
  8.1 1.8 %collective-permute-start.1 = (f32[96,256]{1,0:T(8,128)S(1)}, f32[96,256]{1,0:T(8,128)S(1)}, u32[]{:S(2)}, u32[]{:S(2)}) collective-permute-start(f32[96,256]{1,0:T(8,128)S(1)} %add.17), channel_id=1, source_target_pairs={{0,16},{8,40},{16,0},{24,56},{32,48},{40,8},{48,32},{56,24},{64,80... | collective-permute-start | bytes 294920 | tf_op jit(solution)/shard_map/ppermute | solution.py:498
  9.9 2.3 %collective-permute-done.1 = f32[96,256]{1,0:T(8,128)S(1)} collective-permute-done((f32[96,256]{1,0:T(8,128)S(1)}, f32[96,256]{1,0:T(8,128)S(1)}, u32[]{:S(2)}, u32[]{:S(2)}) %collective-permute-start.1) | collective-permute-done | bytes 98336 | tf_op jit(solution)/shard_map/ppermute | solution.py:498
  12.3 1.4 %collective-permute-start.2 = (f32[96,256]{1,0:T(8,128)S(1)}, f32[96,256]{1,0:T(8,128)S(1)}, u32[]{:S(2)}, u32[]{:S(2)}) collective-permute-start(f32[96,256]{1,0:T(8,128)S(1)} %add.18), channel_id=1, source_target_pairs={{0,32},{8,24},{16,48},{24,8},{32,0},{40,56},{48,16},{56,40},{64,96... | collective-permute-start | bytes 294920 | tf_op jit(solution)/shard_map/ppermute | solution.py:498
  13.6 2.2 %collective-permute-done.2 = f32[96,256]{1,0:T(8,128)S(1)} collective-permute-done((f32[96,256]{1,0:T(8,128)S(1)}, f32[96,256]{1,0:T(8,128)S(1)}, u32[]{:S(2)}, u32[]{:S(2)}) %collective-permute-start.2) | collective-permute-done | bytes 98336 | tf_op jit(solution)/shard_map/ppermute | solution.py:498
  15.8 3.5 %collective-permute-start.3 = (f32[96,256]{1,0:T(8,128)S(1)}, f32[96,256]{1,0:T(8,128)S(1)}, u32[]{:S(2)}, u32[]{:S(2)}) collective-permute-start(f32[96,256]{1,0:T(8,128)S(1)} %add.19), channel_id=1, source_target_pairs={{0,64},{8,72},{16,80},{24,88},{32,96},{40,104},{48,112},{56,120},{... | collective-permute-start | bytes 294920 | tf_op jit(solution)/shard_map/ppermute | solution.py:498
  19.3 0.7 slice.3
  20.0 0.8 dynamic_slice.3
  20.8 1.0 %collective-permute-done.3 = f32[96,256]{1,0:T(8,128)S(1)} collective-permute-done((f32[96,256]{1,0:T(8,128)S(1)}, f32[96,256]{1,0:T(8,128)S(1)}, u32[]{:S(2)}, u32[]{:S(2)}) %collective-permute-start.3) | collective-permute-done | bytes 98336 | tf_op jit(solution)/shard_map/ppermute | solution.py:498
  21.8 2.8 %collective-permute-start.5 = (f32[1,96,256]{2,1,0:T(8,128)S(1)}, f32[1,96,256]{2,1,0:T(8,128)S(1)}, u32[]{:S(2)}, u32[]{:S(2)}) collective-permute-start(f32[1,96,256]{2,1,0:T(8,128)S(1)} %add_bitcast_fusion), channel_id=1, source_target_pairs={{0,8},{8,0},{16,24},{24,16},{32,40},{40,32},{48,56},{56,48},{64,72... | collective-permute-start | bytes 294920 | tf_op jit(solution)/shard_map/ppermute | solution.py:498
  24.6 2.9 %collective-permute-start.4 = (f32[1,96,256]{2,1,0:T(8,128)S(1)}, f32[1,96,256]{2,1,0:T(8,128)S(1)}, u32[]{:S(2)}, u32[]{:S(2)}) collective-permute-start(f32[1,96,256]{2,1,0:T(8,128)S(1)} %add_bitcast_fusion), channel_id=1, source_target_pairs={{0,4},{1,5},{2,6},{3,7},{4,0},{5,1},{6,2},{7,3},{8,12},{9,13},{10,... | collective-permute-start | bytes 294920 | tf_op jit(solution)/shard_map/ppermute | solution.py:498
  27.7 1.4 %picks.1 = (bf16[304,224]{1,0:T(8,128)(2,1)S(1)}, bf16[304,224]{1,0:T(8,128)(2,1)S(1)}, bf16[608,224]{1,0:T(8,128)(2,1)S(1)}, bf16[608,224]{1,0:T(8,128)(2,1)S(1)}) custom-call(s32[2]{0:T(128)S(1)} %pad_add_fusion.scal.refs_6_), custom_call_target="tpu_custom_call" | custom-call | tf_op jit(solution)/shard_map/picks/pallas_call | solution.py:74
  29.1 1.4 %collective-permute-done.4 = f32[1,96,256]{2,1,0:T(8,128)S(1)} collective-permute-done((f32[1,96,256]{2,1,0:T(8,128)S(1)}, f32[1,96,256]{2,1,0:T(8,128)S(1)}, u32[]{:S(2)}, u32[]{:S(2)}) %collective-permute-start.4) | collective-permute-done | bytes 98336 | tf_op jit(solution)/shard_map/ppermute | solution.py:498
  30.5 0.9 %collective-permute-start.7 = (f32[1,96,256]{2,1,0:T(8,128)S(1)}, f32[1,96,256]{2,1,0:T(8,128)S(1)}, u32[]{:S(2)}, u32[]{:S(2)}) collective-permute-start(f32[1,96,256]{2,1,0:T(8,128)S(1)} %collective-permute-done.4), channel_id=1, source_target_pairs={{0,8},{8,0},{16,24},{24,16},{32,40},{40,32},{48,56},{56,48},{64,72... | collective-permute-start | bytes 294920 | tf_op jit(solution)/shard_map/ppermute | solution.py:498
  31.4 2.8 %collective-permute-start.6 = (f32[2,96,256]{2,1,0:T(8,128)S(1)}, f32[2,96,256]{2,1,0:T(8,128)S(1)}, u32[]{:S(2)}, u32[]{:S(2)}) collective-permute-start(f32[2,96,256]{2,1,0:T(8,128)S(1)} %pad_maximum_fusion.1.refs_0_), channel_id=1, source_target_pairs={{0,2},{1,3},{2,0},{3,1},{4,6},{5,7},{6,4},{7,5},{8,10},{9,11},{10,... | collective-permute-start | bytes 589832 | tf_op jit(solution)/shard_map/ppermute | solution.py:498
  34.3 5.7 %early_first.1 = (f32[512,512]{1,0:T(8,128)S(1)}, f32[304,512]{1,0:T(8,128)S(1)}, f32[608,512]{1,0:T(8,128)S(1)}, f32[304,608]{1,0:T(8,128)S(1)}) custom-call(f32[2,96,256]{2,1,0:T(8,128)S(1)} %pad_maximum_fusion.1.refs_0_, f32[2,96,256]{2,1,0:T(8,128)S(1)} %constant_dynamic-update-slice_fusion.refs_1_.refs_6_, ...), custom_call_target="tpu_custom_call" | custom-call | flops 4000000000 | bytes 4194304 | tf_op jit(solution)/shard_map/early_first/pallas_call | solution.py:313
  40.3 1.5 %collective-permute-start.8 = (f32[4,96,256]{2,1,0:T(8,128)S(1)}, f32[4,96,256]{2,1,0:T(8,128)S(1)}, u32[]{:S(2)}, u32[]{:S(2)}) collective-permute-start(f32[4,96,256]{2,1,0:T(8,128)S(1)} %pad_maximum_fusion), channel_id=1, source_target_pairs={{0,1},{1,0},{2,3},{3,2},{4,5},{5,4},{6,7},{7,6},{8,9},{9,8},{10,11... | collective-permute-start | bytes 1179656 | tf_op jit(solution)/shard_map/ppermute | solution.py:498
  41.8 10.5 %early_second.1 = (f32[512,512]{1,0:T(8,128)S(1)}, f32[304,512]{1,0:T(8,128)S(1)}, f32[304,512]{1,0:T(8,128)S(1)}, f32[608,512]{1,0:T(8,128)S(1)}, f32[304,608]{1,0:T(8,128)S(1)}) custom-call(f32[2,96,256]{2,1,0:T(8,128)S(1)} %collective-permute-done.6.refs_0_, f32[2,96,256]{2,1,0:T(8,128)S(1)} %collective-permute-done.9.refs_1_, ...), custom_call_target="tpu_custom_call" | custom-call | flops 4000000000 | bytes 4194304 | tf_op jit(solution)/shard_map/early_second/pallas_call | solution.py:313
  52.3 0.4 collective-permute-start.10
  52.7 1.6 %late_corner.1 = (f32[2,512,512]{2,1,0:T(8,128)S(1)}, bf16[4,512,256]{2,1,0:T(8,128)(2,1)S(1)}, bf16[4,512,256]{2,1,0:T(8,128)(2,1)S(1)}) custom-call(f32[4,96,256]{2,1,0:T(8,128)S(1)} %collective-permute-done.8.c_ref.own), custom_call_target="tpu_custom_call" | custom-call | flops 1000000000 | bytes 4194304 | tf_op jit(solution)/shard_map/late_corner/pallas_call | solution.py:334
  54.3 25.4 %gram_factor.1 = (f32[297,594]{1,0:T(8,128)}, f32[297,512]{1,0:T(8,128)}) custom-call(s32[2]{0:T(128)S(1)} %pad_add_fusion.scal.refs_6_, f32[4,96,256]{2,1,0:T(8,128)S(1)} %collective-permute-done.8.c_ref.own, f32[4,96,256]{2,1,0:T(8,128)S(1)} %collective-permute-done.10.oth, bf16[304,224]{1,0:T(8,128)(2,1)S(1)} %get-tuple-element.51.refs_2_.lr, ...), custom_call_target="tpu_custom_call" | custom-call | tf_op jit(solution)/shard_map/gram_factor/pallas_call | solution.py:468
  (22 shorter events, 1.4 us)
Async XLA Ops:
  0.6 1.2 %copy-start = (bf16[96,4096]{1,0:T(8,128)(2,1)S(1)}, bf16[96,4096]{1,0:T(8,128)(2,1)}, u32[]{:S(2)}) copy-start(bf16[96,4096]{1,0:T(8,128)(2,1)} %param.5) | copy-start | bytes 2359300
  5.7 2.4 %collective-permute-start = (f32[96,256]{1,0:T(8,128)S(1)}, f32[96,256]{1,0:T(8,128)S(1)}, u32[]{:S(2)}, u32[]{:S(2)}) collective-permute-start(f32[96,256]{1,0:T(8,128)S(1)} %get-tuple-element.44), channel_id=1, source_target_pairs={{0,8},{8,0},{16,24},{24,16},{32,40},{40,32},{48,56},{56,48},{64,72... | collective-permute-start | bytes 294920 | tf_op jit(solution)/shard_map/ppermute | solution.py:498
  8.1 4.1 %collective-permute-start.1 = (f32[96,256]{1,0:T(8,128)S(1)}, f32[96,256]{1,0:T(8,128)S(1)}, u32[]{:S(2)}, u32[]{:S(2)}) collective-permute-start(f32[96,256]{1,0:T(8,128)S(1)} %add.17), channel_id=1, source_target_pairs={{0,16},{8,40},{16,0},{24,56},{32,48},{40,8},{48,32},{56,24},{64,80... | collective-permute-start | bytes 294920 | tf_op jit(solution)/shard_map/ppermute | solution.py:498
  12.3 3.5 %collective-permute-start.2 = (f32[96,256]{1,0:T(8,128)S(1)}, f32[96,256]{1,0:T(8,128)S(1)}, u32[]{:S(2)}, u32[]{:S(2)}) collective-permute-start(f32[96,256]{1,0:T(8,128)S(1)} %add.18), channel_id=1, source_target_pairs={{0,32},{8,24},{16,48},{24,8},{32,0},{40,56},{48,16},{56,40},{64,96... | collective-permute-start | bytes 294920 | tf_op jit(solution)/shard_map/ppermute | solution.py:498
  15.8 6.0 %collective-permute-start.3 = (f32[96,256]{1,0:T(8,128)S(1)}, f32[96,256]{1,0:T(8,128)S(1)}, u32[]{:S(2)}, u32[]{:S(2)}) collective-permute-start(f32[96,256]{1,0:T(8,128)S(1)} %add.19), channel_id=1, source_target_pairs={{0,64},{8,72},{16,80},{24,88},{32,96},{40,104},{48,112},{56,120},{... | collective-permute-start | bytes 294920 | tf_op jit(solution)/shard_map/ppermute | solution.py:498
  21.8 7.2 %collective-permute-start.5 = (f32[1,96,256]{2,1,0:T(8,128)S(1)}, f32[1,96,256]{2,1,0:T(8,128)S(1)}, u32[]{:S(2)}, u32[]{:S(2)}) collective-permute-start(f32[1,96,256]{2,1,0:T(8,128)S(1)} %add_bitcast_fusion), channel_id=1, source_target_pairs={{0,8},{8,0},{16,24},{24,16},{32,40},{40,32},{48,56},{56,48},{64,72... | collective-permute-start | bytes 294920 | tf_op jit(solution)/shard_map/ppermute | solution.py:498
  24.6 5.9 %collective-permute-start.4 = (f32[1,96,256]{2,1,0:T(8,128)S(1)}, f32[1,96,256]{2,1,0:T(8,128)S(1)}, u32[]{:S(2)}, u32[]{:S(2)}) collective-permute-start(f32[1,96,256]{2,1,0:T(8,128)S(1)} %add_bitcast_fusion), channel_id=1, source_target_pairs={{0,4},{1,5},{2,6},{3,7},{4,0},{5,1},{6,2},{7,3},{8,12},{9,13},{10,... | collective-permute-start | bytes 294920 | tf_op jit(solution)/shard_map/ppermute | solution.py:498
  30.5 3.7 %collective-permute-start.7 = (f32[1,96,256]{2,1,0:T(8,128)S(1)}, f32[1,96,256]{2,1,0:T(8,128)S(1)}, u32[]{:S(2)}, u32[]{:S(2)}) collective-permute-start(f32[1,96,256]{2,1,0:T(8,128)S(1)} %collective-permute-done.4), channel_id=1, source_target_pairs={{0,8},{8,0},{16,24},{24,16},{32,40},{40,32},{48,56},{56,48},{64,72... | collective-permute-start | bytes 294920 | tf_op jit(solution)/shard_map/ppermute | solution.py:498
  31.4 8.5 %collective-permute-start.6 = (f32[2,96,256]{2,1,0:T(8,128)S(1)}, f32[2,96,256]{2,1,0:T(8,128)S(1)}, u32[]{:S(2)}, u32[]{:S(2)}) collective-permute-start(f32[2,96,256]{2,1,0:T(8,128)S(1)} %pad_maximum_fusion.1.refs_0_), channel_id=1, source_target_pairs={{0,2},{1,3},{2,0},{3,1},{4,6},{5,7},{6,4},{7,5},{8,10},{9,11},{10,... | collective-permute-start | bytes 589832 | tf_op jit(solution)/shard_map/ppermute | solution.py:498
  39.9 1.9 %collective-permute-start.9 = (f32[2,96,256]{2,1,0:T(8,128)S(1)}, f32[2,96,256]{2,1,0:T(8,128)S(1)}, u32[]{:S(2)}, u32[]{:S(2)}) collective-permute-start(f32[2,96,256]{2,1,0:T(8,128)S(1)} %collective-permute-done.6.refs_0_), channel_id=1, source_target_pairs={{0,8},{8,0},{16,24},{24,16},{32,40},{40,32},{48,56},{56,48},{64,72... | collective-permute-start | bytes 589832 | tf_op jit(solution)/shard_map/ppermute | solution.py:498
  40.3 12.0 %collective-permute-start.8 = (f32[4,96,256]{2,1,0:T(8,128)S(1)}, f32[4,96,256]{2,1,0:T(8,128)S(1)}, u32[]{:S(2)}, u32[]{:S(2)}) collective-permute-start(f32[4,96,256]{2,1,0:T(8,128)S(1)} %pad_maximum_fusion), channel_id=1, source_target_pairs={{0,1},{1,0},{2,3},{3,2},{4,5},{5,4},{6,7},{7,6},{8,9},{9,8},{10,11... | collective-permute-start | bytes 1179656 | tf_op jit(solution)/shard_map/ppermute | solution.py:498
  52.3 1.9 %collective-permute-start.10 = (f32[4,96,256]{2,1,0:T(8,128)S(1)}, f32[4,96,256]{2,1,0:T(8,128)S(1)}, u32[]{:S(2)}, u32[]{:S(2)}) collective-permute-start(f32[4,96,256]{2,1,0:T(8,128)S(1)} %collective-permute-done.8.c_ref.own), channel_id=1, source_target_pairs={{0,8},{8,0},{16,24},{24,16},{32,40},{40,32},{48,56},{56,48},{64,72... | collective-permute-start | bytes 1179656 | tf_op jit(solution)/shard_map/ppermute | solution.py:498

commit v3 on v2

--- a/solution.py
+++ b/solution.py
@@ -90,19 +90,24 @@
         a += 1
 
 
+def panel_one(t, c_s, f_ref, fh, fl, modes, scale):
+    panel_features(c_s, t, f_ref, modes, scale)
+    fh[t], fl[t] = split(f_ref[...])
+
+
 def panel_pair(t, c_s, f_s, fh, fl, modes, scale):
     for i in range(2):
-        panel_features(c_s, t + i, f_s.at[i], modes, scale)
-        fh[t + i], fl[t + i] = split(f_s[i])
+        panel_one(t + i, c_s, f_s.at[i], fh, fl, modes, scale)
+
+
+def corner_one(t, fh, fl, at):
+    h, l = fh[t], fl[t]
+    rows = slice(at, at + HALF)
+    return dot3((h[rows], l[rows]), (h[at:], l[at:]))
 
 
 def corner_part(t, fh, fl, at):
-    def one(i):
-        h, l = fh[t + i], fl[t + i]
-        rows = slice(at, at + HALF)
-        return dot3((h[rows], l[rows]), (h[at:], l[at:]))
-
-    return one(0) + one(1)
+    return corner_one(t, fh, fl, at) + corner_one(t + 1, fh, fl, at)
 
 
 def corner_pair(t, fh, fl, a_ref):
@@ -245,53 +250,79 @@
     return jnp.where(ri == ci, values, 0.0)
 
 
+def start_kernel(modes, scale, own, lr, rr, lc, rc, scal, ridge_panel, ridge_cols, a_out, gr, gc, gt, f_s, fh, fl):
+    gc[...] = diagonal(gc.shape, scal[1], 0, ridge_panel[...])
+    gt[...] = diagonal(gt.shape, scal[0], scal[1], ridge_cols[...])
+    panel_one(0, own, f_s, fh, fl, modes, scale)
+    a_out[0:HALF, :] = corner_one(0, fh, fl, 0)
+    a_out[HALF:, HALF:] = corner_one(0, fh, fl, HALF)
+    for part in block_parts(0, own, fh, fl, lr, rr, lc, rc, gr, gc, gt, modes, (None, gc, gt)):
+        part()
+
+
 def early_kernel(modes, scale, first, *refs):
     own, oth, lr, rr, lc, rc = refs[0:6]
     if first:
-        scal, ridge_panel, ridge_cols = refs[6:9]
-        a_out, gr, gc, gt, c_s, f_s, fh, fl, a_s, pair_s = refs[9:]
-        pair_s[...] = jnp.zeros_like(pair_s)
-        gc[...] = diagonal(gc.shape, scal[1], 0, ridge_panel[...])
-        gt[...] = diagonal(gt.shape, scal[0], scal[1], ridge_cols[...])
+        a_in, gr_in, gc_in, gt_in = refs[6:10]
+        a_out, gr, gr_oth, gc, gt, c_s, f_s, fh, fl, a_s, pair_s = refs[10:]
     else:
-        left, gr_in, gc_in, gt_in = refs[6:10]
-        a_out, gr, gr_oth, gc, gt, c_s, f_s, fh, fl, a_s, pair_s = refs[10:]
-        gc[...] = gc_in[...]
-        gt[...] = gt_in[...]
-        pair_s[...] = jnp.zeros_like(pair_s)
-        for i in range(2):
-            c_s[4 + i] = left[i]
-        panel_pair(4, c_s, f_s, fh, fl, modes, scale)
+        left, gr_in, gr_oth_in, gc_in, gt_in = refs[6:11]
+        a_out, gr, gr_oth, gc, gt, c_s, f_s, fh, fl, a_s, pair_s = refs[11:]
     for i in range(2):
         c_s[i] = own[i]
         c_s[2 + i] = oth[i]
 
-    def corner_body(i, carry):
+    def add(t, rows, start):
+        for part in block_parts(t, c_s, fh, fl, lr, rr, lc, rc, rows, gc, gt, modes, start):
+            part()
+
+    if first:
+        panel_one(1, c_s, f_s.at[0], fh, fl, modes, scale)
+        panel_pair(2, c_s, f_s, fh, fl, modes, scale)
+        corner_pair(2, fh, fl, a_out)
+        a_out[0:HALF, :] += a_in[0:HALF, :] + corner_one(1, fh, fl, 0)
+        a_out[HALF:, HALF:] += a_in[HALF:, HALF:] + corner_one(1, fh, fl, HALF)
+        add(1, gr, (gr_in, gc_in, gt_in))
+        add(2, gr_oth, (None, gc, gt))
+        return
+    for i in range(2):
         panel_pair(2 * i, c_s, f_s, fh, fl, modes, scale)
         corner_pair(2 * i, fh, fl, a_s.at[i])
+    a_out[...] = a_s[0] + a_s[1]
+    c_s[4] = left[1]
+    panel_one(4, c_s, f_s.at[0], fh, fl, modes, scale)
+    add(4, gr_oth, (gr_oth_in, gc_in, gt_in))
+
+    def pair_body(i, carry):
+        add(2 * i, pair_s.at[i], (None, gc, gt))
+        add(2 * i + 1, pair_s.at[i], None)
         return carry
 
-    if first:
-        lax.fori_loop(0, 2, corner_body, 0)
-    else:
-        corner_body(0, 0)
-        corner_body(1, 0)
-    a_out[...] = a_s[0] + a_s[1]
-
-    def gram_body(i, carry):
-        together = 1 if first else 3
-        for t in range(together):
-            t = together * i + t
-            for part in block_parts(t, c_s, fh, fl, lr, rr, lc, rc, pair_s.at[t // 2], gc, gt, modes):
-                part()
-        return carry
-
-    lax.fori_loop(0, 2, gram_body, 0)
-    if first:
-        gr[...] = pair_s[0]
-    else:
-        gr[...] = gr_in[...] + pair_s[0]
-        gr_oth[...] = pair_s[2] + pair_s[1]
+    lax.fori_loop(0, 2, pair_body, 0)
+    gr[...] = gr_in[...] + pair_s[0]
+    gr_oth[...] += pair_s[1]
+
+
+def start(own, tables, scal, ridge_panel, ridge_cols, modes, scale):
+    lr, rr, lc, rc = tables
+    row_pad, col_pad = lr.shape[0], lc.shape[0]
+    n = own.shape[2]
+    vmem = pl.BlockSpec(memory_space=pltpu.VMEM)
+    shapes = [(PANEL, PANEL), (row_pad, PANEL), (col_pad, PANEL), (row_pad, col_pad)]
+    return pl.pallas_call(
+        functools.partial(start_kernel, modes, scale),
+        in_specs=[vmem] * 5 + [pl.BlockSpec(memory_space=pltpu.SMEM)] + [vmem] * 2,
+        out_specs=[vmem] * 4,
+        out_shape=[jax.ShapeDtypeStruct(s, F32) for s in shapes],
+        scratch_shapes=[
+            pltpu.VMEM((PANEL, n), F32),
+            pltpu.VMEM((1, PANEL, n), BF16),
+            pltpu.VMEM((1, PANEL, n), BF16),
+        ],
+        compiler_params=pltpu.CompilerParams(vmem_limit_bytes=24 * 2**20),
+        cost_estimate=pl.CostEstimate(flops=10**9, bytes_accessed=2**22, transcendentals=0),
+        name="early_start",
+    )(own, lr, rr, lc, rc, scal, ridge_panel, ridge_cols)
 
 
 def early(own, oth, tables, rest, first, modes, scale, cost):
@@ -299,23 +330,21 @@
     row_pad, col_pad = lr.shape[0], lc.shape[0]
     n = own.shape[2]
     vmem = pl.BlockSpec(memory_space=pltpu.VMEM)
-    smem = pl.BlockSpec(memory_space=pltpu.SMEM)
-    held = 4 if first else 6
-    scratch = [
-        pltpu.VMEM((held, modes, n), F32),
-        pltpu.VMEM((2, PANEL, n), F32),
-        pltpu.VMEM((held, PANEL, n), BF16),
-        pltpu.VMEM((held, PANEL, n), BF16),
-        pltpu.VMEM((2, PANEL, PANEL), F32),
-        pltpu.VMEM((1 if first else 3, row_pad, PANEL), F32),
-    ]
-    shapes = [(PANEL, PANEL)] + [(row_pad, PANEL)] * (1 if first else 2) + [(col_pad, PANEL), (row_pad, col_pad)]
+    held = 4 if first else 5
+    shapes = [(PANEL, PANEL)] + [(row_pad, PANEL)] * 2 + [(col_pad, PANEL), (row_pad, col_pad)]
     return pl.pallas_call(
         functools.partial(early_kernel, modes, scale, first),
-        in_specs=[vmem] * 6 + ([smem, vmem, vmem] if first else [vmem] * 4),
+        in_specs=[vmem] * (6 + len(rest)),
         out_specs=[vmem] * len(shapes),
         out_shape=[jax.ShapeDtypeStruct(s, F32) for s in shapes],
-        scratch_shapes=scratch,
+        scratch_shapes=[
+            pltpu.VMEM((held, modes, n), F32),
+            pltpu.VMEM((2, PANEL, n), F32),
+            pltpu.VMEM((held, PANEL, n), BF16),
+            pltpu.VMEM((held, PANEL, n), BF16),
+            pltpu.VMEM((2, PANEL, PANEL), F32),
+            pltpu.VMEM((2, row_pad, PANEL), F32),
+        ],
         compiler_params=pltpu.CompilerParams(vmem_limit_bytes=32 * 2**20),
         cost_estimate=pl.CostEstimate(flops=cost, bytes_accessed=2**22, transcendentals=0),
         name="early_first" if first else "early_second",
@@ -523,18 +552,22 @@
     offset = lax.dot_general(reference_field[None, :], pod_basis, NT, preferred_element_type=F32)
     keep, send = halves(core[None].astype(jnp.int32), projected, offset)
     total = keep + swap(send, "cells", 1)
+    together = lax.optimization_barrier
     for bit, other_bit in ((2, 4), (4, 2), (8, 8)):
-        total = total + swap(total, "cells", bit, other_bit)
-
-    together = lax.optimization_barrier
+        got = swap(total, "cells", bit, other_bit)
+        if bit == 4:
+            got, tables, ridge_panel, ridge_cols = together((got, tables, ridge_panel, ridge_cols))
+        total = total + got
+
     own0 = total[None]
     own1 = swap(own0, "snap", 4)
     oth0 = swap(own0, "cells", 1)
-    own1, oth0, tables, ridge_panel, ridge_cols = together((own1, oth0, tables, ridge_panel, ridge_cols))
+    sums = start(own0, tables, scal, ridge_panel, ridge_cols, modes, scale)
+    own1, oth0, *sums = together((own1, oth0, *sums))
     pair = jnp.concatenate([own0, own1], 0)
     own2 = swap(pair, "snap", 2)
     oth_pair = jnp.concatenate([oth0, swap(own1, "cells", 1)], 0)
-    sums = early(pair, oth_pair, tables, (scal, ridge_panel, ridge_cols), True, modes, scale, 4 * 10**9)
+    sums = early(pair, oth_pair, tables, sums, True, modes, scale, 4 * 10**9)
     own2, a0, *sums = together((own2, *sums))
     own3 = swap(jnp.concatenate([pair, own2], 0), "snap", 1)
     oth2 = swap(own2, "cells", 1)

time: 80 us -> 79.3 us (level)
  Pallas kernels: 44.7 us -> 43.4 us
  starting transfers between devices: 19.8 us -> 20.7 us
    pallas_call x2, Pallas kernels: 16.1 us -> 12.6 us  [early(): pl.pallas_call(functools.partial(early_kernel, modes, scale, first), in_s...]
    pallas_call x0 -> x1, Pallas kernels: none -> 2.41 us  [start(): pl.pallas_call(functools.partial(start_kernel, modes, scale), in_specs=[v...]
    ppermute x11, starting transfers between devices: 19.8 us -> 20.7 us  [swap(): lax.ppermute(value, axis, [(i, i ^ bits[i & 1]) for i in range(size)])]
  transfers between devices with their start and end apart: 11 -> 11, of which waited for: 5 -> 7; matrix products, arithmetic and copies ran while one was open for 2% -> 2% of each run, Pallas kernels for 24% -> 23%
where the time goes in v3:
time: 79.3 us; the launch traced here: 79 us
  Pallas kernels  43.4 us (55%)
  starting transfers between devices  20.7 us (26%)
  waiting for transfers between devices  7.63 us (10%)
  matrix products  3.75 us (5%)
  local copies, waits for them, and re-layouts  2.62 us (3%)
    pallas_call x1, Pallas kernels, main(): pl.pallas_call(functools.partial(main_kernel, modes, scale), in_specs=[pl...  25.3 us
    ppermute x11, starting transfers between devices, swap(): lax.ppermute(value, axis, [(i, i ^ bits[i & 1]) for i in range(size)])  20.7 us
    pallas_call x2, Pallas kernels, early(): pl.pallas_call(functools.partial(early_kernel, modes, scale, first), in_s...  12.6 us
    ppermute x11, waiting for transfers between devices, swap(): lax.ppermute(value, axis, [(i, i ^ bits[i & 1]) for i in range(size)])  7.63 us
    dot_general x1, matrix products, per_device(): lax.dot_general(snapshots, pod_basis, NT, preferred_element_type=F32)  3.45 us
    pallas_call x1, Pallas kernels, start(): pl.pallas_call(functools.partial(start_kernel, modes, scale), in_specs=[v...  2.41 us
  transfers between devices with their start and end apart: 11, of which 7 were waited for; matrix products, arithmetic and copies ran while one was open for 2% of the time, Pallas kernels for 23%

profile of v3, /device:TPU:1, one launch (start us, length us, event | category | flops | bytes accessed | tf_op | source)
XLA Modules:
  0.0 79.0 jit_solution(13922756011107734706)
XLA Ops:
  0.7 0.8 reshape.7
  2.1 3.5 %fusion.part = f32[512,96]{1,0:T(8,128)S(1)} fusion(bf16[512,4096]{1,0:T(8,128)(2,1)} %param.4, bf16[96,4096]{1,0:T(8,128)(2,1)S(1)} %copy-done), kind=kOutput, calls=%fused_computation.6 | convolution fusion | flops 402653184 | bytes 5177344 | tf_op jit(solution)/shard_map/dot_general | solution.py:551
  5.7 1.5 %collective-permute-start = (f32[96,256]{1,0:T(8,128)S(1)}, f32[96,256]{1,0:T(8,128)S(1)}, u32[]{:S(2)}, u32[]{:S(2)}) collective-permute-start(f32[96,256]{1,0:T(8,128)S(1)} %get-tuple-element.55), channel_id=1, source_target_pairs={{0,8},{8,0},{16,24},{24,16},{32,40},{40,32},{48,56},{56,48},{64,72... | collective-permute-start | bytes 294920 | tf_op jit(solution)/shard_map/ppermute | solution.py:527
  7.2 0.9 %collective-permute-done = f32[96,256]{1,0:T(8,128)S(1)} collective-permute-done((f32[96,256]{1,0:T(8,128)S(1)}, f32[96,256]{1,0:T(8,128)S(1)}, u32[]{:S(2)}, u32[]{:S(2)}) %collective-permute-start) | collective-permute-done | bytes 98336 | tf_op jit(solution)/shard_map/ppermute | solution.py:527
  8.1 1.8 %collective-permute-start.1 = (f32[96,256]{1,0:T(8,128)S(1)}, f32[96,256]{1,0:T(8,128)S(1)}, u32[]{:S(2)}, u32[]{:S(2)}) collective-permute-start(f32[96,256]{1,0:T(8,128)S(1)} %add.17), channel_id=1, source_target_pairs={{0,16},{8,40},{16,0},{24,56},{32,48},{40,8},{48,32},{56,24},{64,80... | collective-permute-start | bytes 294920 | tf_op jit(solution)/shard_map/ppermute | solution.py:527
  11.4 0.8 %collective-permute-done.1 = f32[96,256]{1,0:T(8,128)S(1)} collective-permute-done((f32[96,256]{1,0:T(8,128)S(1)}, f32[96,256]{1,0:T(8,128)S(1)}, u32[]{:S(2)}, u32[]{:S(2)}) %collective-permute-start.1) | collective-permute-done | bytes 98336 | tf_op jit(solution)/shard_map/ppermute | solution.py:527
  12.3 1.4 %collective-permute-start.2 = (f32[96,256]{1,0:T(8,128)S(1)}, f32[96,256]{1,0:T(8,128)S(1)}, u32[]{:S(2)}, u32[]{:S(2)}) collective-permute-start(f32[96,256]{1,0:T(8,128)S(1)} %add.18), channel_id=1, source_target_pairs={{0,32},{8,24},{16,48},{24,8},{32,0},{40,56},{48,16},{56,40},{64,96... | collective-permute-start | bytes 294920 | tf_op jit(solution)/shard_map/ppermute | solution.py:527
  13.7 1.4 %picks.1 = (bf16[304,224]{1,0:T(8,128)(2,1)S(1)}, bf16[304,224]{1,0:T(8,128)(2,1)S(1)}, bf16[608,224]{1,0:T(8,128)(2,1)S(1)}, bf16[608,224]{1,0:T(8,128)(2,1)S(1)}) custom-call(s32[2]{0:T(128)S(1)} %pad_add_fusion.scal), custom_call_target="tpu_custom_call" | custom-call | tf_op jit(solution)/shard_map/picks/pallas_call | solution.py:74
  15.8 3.5 %collective-permute-start.3 = (f32[96,256]{1,0:T(8,128)S(1)}, f32[96,256]{1,0:T(8,128)S(1)}, u32[]{:S(2)}, u32[]{:S(2)}) collective-permute-start(f32[96,256]{1,0:T(8,128)S(1)} %add.20), channel_id=1, source_target_pairs={{0,64},{8,72},{16,80},{24,88},{32,96},{40,104},{48,112},{56,120},{... | collective-permute-start | bytes 294920 | tf_op jit(solution)/shard_map/ppermute | solution.py:527
  19.3 2.5 %collective-permute-done.3 = f32[96,256]{1,0:T(8,128)S(1)} collective-permute-done((f32[96,256]{1,0:T(8,128)S(1)}, f32[96,256]{1,0:T(8,128)S(1)}, u32[]{:S(2)}, u32[]{:S(2)}) %collective-permute-start.3) | collective-permute-done | bytes 98336 | tf_op jit(solution)/shard_map/ppermute | solution.py:527
  21.8 2.8 %collective-permute-start.5 = (f32[1,96,256]{2,1,0:T(8,128)S(1)}, f32[1,96,256]{2,1,0:T(8,128)S(1)}, u32[]{:S(2)}, u32[]{:S(2)}) collective-permute-start(f32[1,96,256]{2,1,0:T(8,128)S(1)} %add_bitcast_fusion.own), channel_id=1, source_target_pairs={{0,8},{8,0},{16,24},{24,16},{32,40},{40,32},{48,56},{56,48},{64,72... | collective-permute-start | bytes 294920 | tf_op jit(solution)/shard_map/ppermute | solution.py:527
  24.6 2.9 %collective-permute-start.4 = (f32[1,96,256]{2,1,0:T(8,128)S(1)}, f32[1,96,256]{2,1,0:T(8,128)S(1)}, u32[]{:S(2)}, u32[]{:S(2)}) collective-permute-start(f32[1,96,256]{2,1,0:T(8,128)S(1)} %add_bitcast_fusion.own), channel_id=1, source_target_pairs={{0,4},{1,5},{2,6},{3,7},{4,0},{5,1},{6,2},{7,3},{8,12},{9,13},{10,... | collective-permute-start | bytes 294920 | tf_op jit(solution)/shard_map/ppermute | solution.py:527
  27.6 2.4 %early_start.1 = (f32[512,512]{1,0:T(8,128)S(1)}, f32[304,512]{1,0:T(8,128)S(1)}, f32[608,512]{1,0:T(8,128)S(1)}, f32[304,608]{1,0:T(8,128)S(1)}) custom-call(f32[1,96,256]{2,1,0:T(8,128)S(1)} %add_bitcast_fusion.own, bf16[304,224]{1,0:T(8,128)(2,1)S(1)} %get-tuple-element.61.lr.refs_2_, bf16[304,224]{1,0:T(8,128)(2,1)S(1)} %get-tuple-element.62.rr.refs_3_, ...), custom_call_target="tpu_custom_call" | custom-call | flops 1000000000 | bytes 4194304 | tf_op jit(solution)/shard_map/early_start/pallas_call | solution.py:312
  30.5 0.9 %collective-permute-start.7 = (f32[1,96,256]{2,1,0:T(8,128)S(1)}, f32[1,96,256]{2,1,0:T(8,128)S(1)}, u32[]{:S(2)}, u32[]{:S(2)}) collective-permute-start(f32[1,96,256]{2,1,0:T(8,128)S(1)} %collective-permute-done.4), channel_id=1, source_target_pairs={{0,8},{8,0},{16,24},{24,16},{32,40},{40,32},{48,56},{56,48},{64,72... | collective-permute-start | bytes 294920 | tf_op jit(solution)/shard_map/ppermute | solution.py:527
  31.4 2.8 %collective-permute-start.6 = (f32[2,96,256]{2,1,0:T(8,128)S(1)}, f32[2,96,256]{2,1,0:T(8,128)S(1)}, u32[]{:S(2)}, u32[]{:S(2)}) collective-permute-start(f32[2,96,256]{2,1,0:T(8,128)S(1)} %pad_maximum_fusion.1.refs_0_), channel_id=1, source_target_pairs={{0,2},{1,3},{2,0},{3,1},{4,6},{5,7},{6,4},{7,5},{8,10},{9,11},{10,... | collective-permute-start | bytes 589832 | tf_op jit(solution)/shard_map/ppermute | solution.py:527
  34.3 3.9 %early_first.1 = (f32[512,512]{1,0:T(8,128)S(1)}, f32[304,512]{1,0:T(8,128)S(1)}, f32[304,512]{1,0:T(8,128)S(1)}, f32[608,512]{1,0:T(8,128)S(1)}, f32[304,608]{1,0:T(8,128)S(1)}) custom-call(f32[2,96,256]{2,1,0:T(8,128)S(1)} %pad_maximum_fusion.1.refs_0_, f32[2,96,256]{2,1,0:T(8,128)S(1)} %constant_dynamic-update-slice_fusion.refs_1_.refs_6_, ...), custom_call_target="tpu_custom_call" | custom-call | flops 4000000000 | bytes 4194304 | tf_op jit(solution)/shard_map/early_first/pallas_call | solution.py:335
  38.1 1.4 %collective-permute-done.6.refs_0_ = f32[2,96,256]{2,1,0:T(8,128)S(1)} collective-permute-done((f32[2,96,256]{2,1,0:T(8,128)S(1)}, f32[2,96,256]{2,1,0:T(8,128)S(1)}, u32[]{:S(2)}, u32[]{:S(2)}) %collective-permute-start.6) | collective-permute-done | bytes 196640 | tf_op jit(solution)/shard_map/ppermute | solution.py:527
  39.5 0.8 collective-permute-start.9
  40.3 1.5 %collective-permute-start.8 = (f32[4,96,256]{2,1,0:T(8,128)S(1)}, f32[4,96,256]{2,1,0:T(8,128)S(1)}, u32[]{:S(2)}, u32[]{:S(2)}) collective-permute-start(f32[4,96,256]{2,1,0:T(8,128)S(1)} %pad_maximum_fusion), channel_id=1, source_target_pairs={{0,1},{1,0},{2,3},{3,2},{4,5},{5,4},{6,7},{7,6},{8,9},{9,8},{10,11... | collective-permute-start | bytes 1179656 | tf_op jit(solution)/shard_map/ppermute | solution.py:527
  41.8 8.7 %early_second.1 = (f32[512,512]{1,0:T(8,128)S(1)}, f32[304,512]{1,0:T(8,128)S(1)}, f32[304,512]{1,0:T(8,128)S(1)}, f32[608,512]{1,0:T(8,128)S(1)}, f32[304,608]{1,0:T(8,128)S(1)}) custom-call(f32[2,96,256]{2,1,0:T(8,128)S(1)} %collective-permute-done.6.refs_0_, f32[2,96,256]{2,1,0:T(8,128)S(1)} %collective-permute-done.9.refs_1_, ...), custom_call_target="tpu_custom_call" | custom-call | flops 4000000000 | bytes 4194304 | tf_op jit(solution)/shard_map/early_second/pallas_call | solution.py:335
  50.6 0.8 collective-permute-done.8.c_ref.own
  51.3 0.8 collective-permute-start.10
  52.1 1.5 %late_corner.1 = (f32[2,512,512]{2,1,0:T(8,128)S(1)}, bf16[4,512,256]{2,1,0:T(8,128)(2,1)S(1)}, bf16[4,512,256]{2,1,0:T(8,128)(2,1)S(1)}) custom-call(f32[4,96,256]{2,1,0:T(8,128)S(1)} %collective-permute-done.8.c_ref.own), custom_call_target="tpu_custom_call" | custom-call | flops 1000000000 | bytes 4194304 | tf_op jit(solution)/shard_map/late_corner/pallas_call | solution.py:363
  53.7 25.3 %gram_factor.1 = (f32[297,594]{1,0:T(8,128)}, f32[297,512]{1,0:T(8,128)}) custom-call(s32[2]{0:T(128)S(1)} %pad_add_fusion.scal, f32[4,96,256]{2,1,0:T(8,128)S(1)} %collective-permute-done.8.c_ref.own, f32[4,96,256]{2,1,0:T(8,128)S(1)} %collective-permute-done.10.oth, bf16[304,224]{1,0:T(8,128)(2,1)S(1)} %get-tuple-element.61.lr.refs_2_, ...), custom_call_target="tpu_custom_call" | custom-call | tf_op jit(solution)/shard_map/gram_factor/pallas_call | solution.py:497
  (23 shorter events, 3.6 us)
Async XLA Ops:
  0.6 1.2 %copy-start = (bf16[96,4096]{1,0:T(8,128)(2,1)S(1)}, bf16[96,4096]{1,0:T(8,128)(2,1)}, u32[]{:S(2)}) copy-start(bf16[96,4096]{1,0:T(8,128)(2,1)} %param.5) | copy-start | bytes 2359300
  5.7 2.4 %collective-permute-start = (f32[96,256]{1,0:T(8,128)S(1)}, f32[96,256]{1,0:T(8,128)S(1)}, u32[]{:S(2)}, u32[]{:S(2)}) collective-permute-start(f32[96,256]{1,0:T(8,128)S(1)} %get-tuple-element.55), channel_id=1, source_target_pairs={{0,8},{8,0},{16,24},{24,16},{32,40},{40,32},{48,56},{56,48},{64,72... | collective-permute-start | bytes 294920 | tf_op jit(solution)/shard_map/ppermute | solution.py:527
  8.1 4.1 %collective-permute-start.1 = (f32[96,256]{1,0:T(8,128)S(1)}, f32[96,256]{1,0:T(8,128)S(1)}, u32[]{:S(2)}, u32[]{:S(2)}) collective-permute-start(f32[96,256]{1,0:T(8,128)S(1)} %add.17), channel_id=1, source_target_pairs={{0,16},{8,40},{16,0},{24,56},{32,48},{40,8},{48,32},{56,24},{64,80... | collective-permute-start | bytes 294920 | tf_op jit(solution)/shard_map/ppermute | solution.py:527
  12.3 3.5 %collective-permute-start.2 = (f32[96,256]{1,0:T(8,128)S(1)}, f32[96,256]{1,0:T(8,128)S(1)}, u32[]{:S(2)}, u32[]{:S(2)}) collective-permute-start(f32[96,256]{1,0:T(8,128)S(1)} %add.18), channel_id=1, source_target_pairs={{0,32},{8,24},{16,48},{24,8},{32,0},{40,56},{48,16},{56,40},{64,96... | collective-permute-start | bytes 294920 | tf_op jit(solution)/shard_map/ppermute | solution.py:527
  15.8 6.0 %collective-permute-start.3 = (f32[96,256]{1,0:T(8,128)S(1)}, f32[96,256]{1,0:T(8,128)S(1)}, u32[]{:S(2)}, u32[]{:S(2)}) collective-permute-start(f32[96,256]{1,0:T(8,128)S(1)} %add.20), channel_id=1, source_target_pairs={{0,64},{8,72},{16,80},{24,88},{32,96},{40,104},{48,112},{56,120},{... | collective-permute-start | bytes 294920 | tf_op jit(solution)/shard_map/ppermute | solution.py:527
  21.8 8.2 %collective-permute-start.5 = (f32[1,96,256]{2,1,0:T(8,128)S(1)}, f32[1,96,256]{2,1,0:T(8,128)S(1)}, u32[]{:S(2)}, u32[]{:S(2)}) collective-permute-start(f32[1,96,256]{2,1,0:T(8,128)S(1)} %add_bitcast_fusion.own), channel_id=1, source_target_pairs={{0,8},{8,0},{16,24},{24,16},{32,40},{40,32},{48,56},{56,48},{64,72... | collective-permute-start | bytes 294920 | tf_op jit(solution)/shard_map/ppermute | solution.py:527
  24.6 5.9 %collective-permute-start.4 = (f32[1,96,256]{2,1,0:T(8,128)S(1)}, f32[1,96,256]{2,1,0:T(8,128)S(1)}, u32[]{:S(2)}, u32[]{:S(2)}) collective-permute-start(f32[1,96,256]{2,1,0:T(8,128)S(1)} %add_bitcast_fusion.own), channel_id=1, source_target_pairs={{0,4},{1,5},{2,6},{3,7},{4,0},{5,1},{6,2},{7,3},{8,12},{9,13},{10,... | collective-permute-start | bytes 294920 | tf_op jit(solution)/shard_map/ppermute | solution.py:527
  30.5 3.7 %collective-permute-start.7 = (f32[1,96,256]{2,1,0:T(8,128)S(1)}, f32[1,96,256]{2,1,0:T(8,128)S(1)}, u32[]{:S(2)}, u32[]{:S(2)}) collective-permute-start(f32[1,96,256]{2,1,0:T(8,128)S(1)} %collective-permute-done.4), channel_id=1, source_target_pairs={{0,8},{8,0},{16,24},{24,16},{32,40},{40,32},{48,56},{56,48},{64,72... | collective-permute-start | bytes 294920 | tf_op jit(solution)/shard_map/ppermute | solution.py:527
  31.4 8.1 %collective-permute-start.6 = (f32[2,96,256]{2,1,0:T(8,128)S(1)}, f32[2,96,256]{2,1,0:T(8,128)S(1)}, u32[]{:S(2)}, u32[]{:S(2)}) collective-permute-start(f32[2,96,256]{2,1,0:T(8,128)S(1)} %pad_maximum_fusion.1.refs_0_), channel_id=1, source_target_pairs={{0,2},{1,3},{2,0},{3,1},{4,6},{5,7},{6,4},{7,5},{8,10},{9,11},{10,... | collective-permute-start | bytes 589832 | tf_op jit(solution)/shard_map/ppermute | solution.py:527
  39.5 2.3 %collective-permute-start.9 = (f32[2,96,256]{2,1,0:T(8,128)S(1)}, f32[2,96,256]{2,1,0:T(8,128)S(1)}, u32[]{:S(2)}, u32[]{:S(2)}) collective-permute-start(f32[2,96,256]{2,1,0:T(8,128)S(1)} %collective-permute-done.6.refs_0_), channel_id=1, source_target_pairs={{0,8},{8,0},{16,24},{24,16},{32,40},{40,32},{48,56},{56,48},{64,72... | collective-permute-start | bytes 589832 | tf_op jit(solution)/shard_map/ppermute | solution.py:527
  40.3 11.0 %collective-permute-start.8 = (f32[4,96,256]{2,1,0:T(8,128)S(1)}, f32[4,96,256]{2,1,0:T(8,128)S(1)}, u32[]{:S(2)}, u32[]{:S(2)}) collective-permute-start(f32[4,96,256]{2,1,0:T(8,128)S(1)} %pad_maximum_fusion), channel_id=1, source_target_pairs={{0,1},{1,0},{2,3},{3,2},{4,5},{5,4},{6,7},{7,6},{8,9},{9,8},{10,11... | collective-permute-start | bytes 1179656 | tf_op jit(solution)/shard_map/ppermute | solution.py:527
  51.3 2.3 %collective-permute-start.10 = (f32[4,96,256]{2,1,0:T(8,128)S(1)}, f32[4,96,256]{2,1,0:T(8,128)S(1)}, u32[]{:S(2)}, u32[]{:S(2)}) collective-permute-start(f32[4,96,256]{2,1,0:T(8,128)S(1)} %collective-permute-done.8.c_ref.own), channel_id=1, source_target_pairs={{0,8},{8,0},{16,24},{24,16},{32,40},{40,32},{48,56},{56,48},{64,72... | collective-permute-start | bytes 1179656 | tf_op jit(solution)/shard_map/ppermute | solution.py:527

commit v4 on v3

--- a/solution.py
+++ b/solution.py
@@ -266,8 +266,8 @@
         a_in, gr_in, gc_in, gt_in = refs[6:10]
         a_out, gr, gr_oth, gc, gt, c_s, f_s, fh, fl, a_s, pair_s = refs[10:]
     else:
-        left, gr_in, gr_oth_in, gc_in, gt_in = refs[6:11]
-        a_out, gr, gr_oth, gc, gt, c_s, f_s, fh, fl, a_s, pair_s = refs[11:]
+        gr_in, gr_oth_in, gc_in, gt_in = refs[6:10]
+        a_out, gr, gr_oth, gc, gt, c_s, f_s, fh, fl, a_s, pair_s = refs[10:]
     for i in range(2):
         c_s[i] = own[i]
         c_s[2 + i] = oth[i]
@@ -284,14 +284,14 @@
         a_out[HALF:, HALF:] += a_in[HALF:, HALF:] + corner_one(1, fh, fl, HALF)
         add(1, gr, (gr_in, gc_in, gt_in))
         add(2, gr_oth, (None, gc, gt))
+        add(3, gr_oth, None)
         return
     for i in range(2):
         panel_pair(2 * i, c_s, f_s, fh, fl, modes, scale)
         corner_pair(2 * i, fh, fl, a_s.at[i])
     a_out[...] = a_s[0] + a_s[1]
-    c_s[4] = left[1]
-    panel_one(4, c_s, f_s.at[0], fh, fl, modes, scale)
-    add(4, gr_oth, (gr_oth_in, gc_in, gt_in))
+    gc[...] = gc_in[...]
+    gt[...] = gt_in[...]
 
     def pair_body(i, carry):
         add(2 * i, pair_s.at[i], (None, gc, gt))
@@ -300,7 +300,7 @@
 
     lax.fori_loop(0, 2, pair_body, 0)
     gr[...] = gr_in[...] + pair_s[0]
-    gr_oth[...] += pair_s[1]
+    gr_oth[...] = gr_oth_in[...] + pair_s[1]
 
 
 def start(own, tables, scal, ridge_panel, ridge_cols, modes, scale):
@@ -330,7 +330,7 @@
     row_pad, col_pad = lr.shape[0], lc.shape[0]
     n = own.shape[2]
     vmem = pl.BlockSpec(memory_space=pltpu.VMEM)
-    held = 4 if first else 5
+    held = 4
     shapes = [(PANEL, PANEL)] + [(row_pad, PANEL)] * 2 + [(col_pad, PANEL), (row_pad, col_pad)]
     return pl.pallas_call(
         functools.partial(early_kernel, modes, scale, first),
@@ -568,11 +568,13 @@
     own2 = swap(pair, "snap", 2)
     oth_pair = jnp.concatenate([oth0, swap(own1, "cells", 1)], 0)
     sums = early(pair, oth_pair, tables, sums, True, modes, scale, 4 * 10**9)
-    own2, a0, *sums = together((own2, *sums))
-    own3 = swap(jnp.concatenate([pair, own2], 0), "snap", 1)
+    near = swap(pair, "snap", 1)
+    own2, near, a0, *sums = together((own2, near, *sums))
+    far = swap(own2, "snap", 1)
     oth2 = swap(own2, "cells", 1)
-    sums = early(own2, oth2, tables, (oth_pair, *sums), False, modes, scale, 4 * 10**9)
-    own3, a1, *sums = together((own3, *sums))
+    sums = early(own2, oth2, tables, sums, False, modes, scale, 4 * 10**9)
+    far, a1, *sums = together((far, *sums))
+    own3 = jnp.concatenate([near, far], 0)
     oth3 = swap(own3, "cells", 1)
     a_own, own_h, own_l = corner_of(own3, modes, scale)
     oth3, a_own, own_h, own_l = together((oth3, a_own, own_h, own_l))

time: 79.3 us -> 81.2 us (1.024)
  waiting for transfers between devices: 7.63 us -> 10.6 us
  starting transfers between devices: 20.7 us -> 19.8 us
    ppermute x11 -> x12, waiting for transfers between devices: 7.63 us -> 10.6 us  [swap(): lax.ppermute(value, axis, [(i, i ^ bits[i & 1]) for i in range(size)])]
    ppermute x11 -> x12, starting transfers between devices: 20.7 us -> 19.8 us  [swap(): lax.ppermute(value, axis, [(i, i ^ bits[i & 1]) for i in range(size)])]
  transfers between devices with their start and end apart: 11 -> 12, of which waited for: 7 -> 7; matrix products, arithmetic and copies ran while one was open for 2% -> 2% of each run, Pallas kernels for 23% -> 22%
where the time goes in v4:
time: 81.2 us; the launch traced here: 80.9 us
  Pallas kernels  43.3 us (53%)
  starting transfers between devices  19.8 us (24%)
  waiting for transfers between devices  10.6 us (13%)
  matrix products  3.75 us (5%)
  local copies, waits for them, and re-layouts  2.64 us (3%)
    pallas_call x1, Pallas kernels, main(): pl.pallas_call(functools.partial(main_kernel, modes, scale), in_specs=[pl...  25.2 us
    ppermute x12, starting transfers between devices, swap(): lax.ppermute(value, axis, [(i, i ^ bits[i & 1]) for i in range(size)])  19.8 us
    pallas_call x2, Pallas kernels, early(): pl.pallas_call(functools.partial(early_kernel, modes, scale, first), in_s...  12.6 us
    ppermute x12, waiting for transfers between devices, swap(): lax.ppermute(value, axis, [(i, i ^ bits[i & 1]) for i in range(size)])  10.6 us
    dot_general x1, matrix products, per_device(): lax.dot_general(snapshots, pod_basis, NT, preferred_element_type=F32)  3.45 us
    pallas_call x1, Pallas kernels, start(): pl.pallas_call(functools.partial(start_kernel, modes, scale), in_specs=[v...  2.41 us
  transfers between devices with their start and end apart: 12, of which 7 were waited for; matrix products, arithmetic and copies ran while one was open for 2% of the time, Pallas kernels for 22%

profile of v4, /device:TPU:1, one launch (start us, length us, event | category | flops | bytes accessed | tf_op | source)
XLA Modules:
  0.0 80.9 jit_solution(3884206574910980063)
XLA Ops:
  0.7 0.8 reshape.7
  2.1 3.5 %fusion.part = f32[512,96]{1,0:T(8,128)S(1)} fusion(bf16[512,4096]{1,0:T(8,128)(2,1)} %param.4, bf16[96,4096]{1,0:T(8,128)(2,1)S(1)} %copy-done), kind=kOutput, calls=%fused_computation.6 | convolution fusion | flops 402653184 | bytes 5177344 | tf_op jit(solution)/shard_map/dot_general | solution.py:551
  5.7 1.5 %collective-permute-start = (f32[96,256]{1,0:T(8,128)S(1)}, f32[96,256]{1,0:T(8,128)S(1)}, u32[]{:S(2)}, u32[]{:S(2)}) collective-permute-start(f32[96,256]{1,0:T(8,128)S(1)} %get-tuple-element.56), channel_id=1, source_target_pairs={{0,8},{8,0},{16,24},{24,16},{32,40},{40,32},{48,56},{56,48},{64,72... | collective-permute-start | bytes 294920 | tf_op jit(solution)/shard_map/ppermute | solution.py:527
  7.2 0.9 %collective-permute-done = f32[96,256]{1,0:T(8,128)S(1)} collective-permute-done((f32[96,256]{1,0:T(8,128)S(1)}, f32[96,256]{1,0:T(8,128)S(1)}, u32[]{:S(2)}, u32[]{:S(2)}) %collective-permute-start) | collective-permute-done | bytes 98336 | tf_op jit(solution)/shard_map/ppermute | solution.py:527
  8.1 1.8 %collective-permute-start.1 = (f32[96,256]{1,0:T(8,128)S(1)}, f32[96,256]{1,0:T(8,128)S(1)}, u32[]{:S(2)}, u32[]{:S(2)}) collective-permute-start(f32[96,256]{1,0:T(8,128)S(1)} %add.17), channel_id=1, source_target_pairs={{0,16},{8,40},{16,0},{24,56},{32,48},{40,8},{48,32},{56,24},{64,80... | collective-permute-start | bytes 294920 | tf_op jit(solution)/shard_map/ppermute | solution.py:527
  10.6 0.8 dynamic_slice.3
  11.4 0.8 %collective-permute-done.1 = f32[96,256]{1,0:T(8,128)S(1)} collective-permute-done((f32[96,256]{1,0:T(8,128)S(1)}, f32[96,256]{1,0:T(8,128)S(1)}, u32[]{:S(2)}, u32[]{:S(2)}) %collective-permute-start.1) | collective-permute-done | bytes 98336 | tf_op jit(solution)/shard_map/ppermute | solution.py:527
  12.3 1.4 %collective-permute-start.2 = (f32[96,256]{1,0:T(8,128)S(1)}, f32[96,256]{1,0:T(8,128)S(1)}, u32[]{:S(2)}, u32[]{:S(2)}) collective-permute-start(f32[96,256]{1,0:T(8,128)S(1)} %add.18), channel_id=1, source_target_pairs={{0,32},{8,24},{16,48},{24,8},{32,0},{40,56},{48,16},{56,40},{64,96... | collective-permute-start | bytes 294920 | tf_op jit(solution)/shard_map/ppermute | solution.py:527
  13.7 1.4 %picks.1 = (bf16[304,224]{1,0:T(8,128)(2,1)S(1)}, bf16[304,224]{1,0:T(8,128)(2,1)S(1)}, bf16[608,224]{1,0:T(8,128)(2,1)S(1)}, bf16[608,224]{1,0:T(8,128)(2,1)S(1)}) custom-call(s32[2]{0:T(128)S(1)} %pad_add_fusion.scal), custom_call_target="tpu_custom_call" | custom-call | tf_op jit(solution)/shard_map/picks/pallas_call | solution.py:74
  15.8 3.5 %collective-permute-start.3 = (f32[96,256]{1,0:T(8,128)S(1)}, f32[96,256]{1,0:T(8,128)S(1)}, u32[]{:S(2)}, u32[]{:S(2)}) collective-permute-start(f32[96,256]{1,0:T(8,128)S(1)} %add.20), channel_id=1, source_target_pairs={{0,64},{8,72},{16,80},{24,88},{32,96},{40,104},{48,112},{56,120},{... | collective-permute-start | bytes 294920 | tf_op jit(solution)/shard_map/ppermute | solution.py:527
  19.3 2.5 %collective-permute-done.3 = f32[96,256]{1,0:T(8,128)S(1)} collective-permute-done((f32[96,256]{1,0:T(8,128)S(1)}, f32[96,256]{1,0:T(8,128)S(1)}, u32[]{:S(2)}, u32[]{:S(2)}) %collective-permute-start.3) | collective-permute-done | bytes 98336 | tf_op jit(solution)/shard_map/ppermute | solution.py:527
  21.8 2.8 %collective-permute-start.5 = (f32[1,96,256]{2,1,0:T(8,128)S(1)}, f32[1,96,256]{2,1,0:T(8,128)S(1)}, u32[]{:S(2)}, u32[]{:S(2)}) collective-permute-start(f32[1,96,256]{2,1,0:T(8,128)S(1)} %add_bitcast_fusion.own), channel_id=1, source_target_pairs={{0,8},{8,0},{16,24},{24,16},{32,40},{40,32},{48,56},{56,48},{64,72... | collective-permute-start | bytes 294920 | tf_op jit(solution)/shard_map/ppermute | solution.py:527
  24.6 2.9 %collective-permute-start.4 = (f32[1,96,256]{2,1,0:T(8,128)S(1)}, f32[1,96,256]{2,1,0:T(8,128)S(1)}, u32[]{:S(2)}, u32[]{:S(2)}) collective-permute-start(f32[1,96,256]{2,1,0:T(8,128)S(1)} %add_bitcast_fusion.own), channel_id=1, source_target_pairs={{0,4},{1,5},{2,6},{3,7},{4,0},{5,1},{6,2},{7,3},{8,12},{9,13},{10,... | collective-permute-start | bytes 294920 | tf_op jit(solution)/shard_map/ppermute | solution.py:527
  27.6 2.4 %early_start.1 = (f32[512,512]{1,0:T(8,128)S(1)}, f32[304,512]{1,0:T(8,128)S(1)}, f32[608,512]{1,0:T(8,128)S(1)}, f32[304,608]{1,0:T(8,128)S(1)}) custom-call(f32[1,96,256]{2,1,0:T(8,128)S(1)} %add_bitcast_fusion.own, bf16[304,224]{1,0:T(8,128)(2,1)S(1)} %get-tuple-element.62.lr.refs_2_, bf16[304,224]{1,0:T(8,128)(2,1)S(1)} %get-tuple-element.63.rr.refs_3_, ...), custom_call_target="tpu_custom_call" | custom-call | flops 1000000000 | bytes 4194304 | tf_op jit(solution)/shard_map/early_start/pallas_call | solution.py:312
  30.5 0.9 %collective-permute-start.8 = (f32[1,96,256]{2,1,0:T(8,128)S(1)}, f32[1,96,256]{2,1,0:T(8,128)S(1)}, u32[]{:S(2)}, u32[]{:S(2)}) collective-permute-start(f32[1,96,256]{2,1,0:T(8,128)S(1)} %collective-permute-done.4), channel_id=1, source_target_pairs={{0,8},{8,0},{16,24},{24,16},{32,40},{40,32},{48,56},{56,48},{64,72... | collective-permute-start | bytes 294920 | tf_op jit(solution)/shard_map/ppermute | solution.py:527
  31.4 1.3 %collective-permute-start.7 = (f32[2,96,256]{2,1,0:T(8,128)S(1)}, f32[2,96,256]{2,1,0:T(8,128)S(1)}, u32[]{:S(2)}, u32[]{:S(2)}) collective-permute-start(f32[2,96,256]{2,1,0:T(8,128)S(1)} %pad_maximum_fusion.refs_0_), channel_id=1, source_target_pairs={{0,1},{1,0},{2,3},{3,2},{4,5},{5,4},{6,7},{7,6},{8,9},{9,8},{10,11... | collective-permute-start | bytes 589832 | tf_op jit(solution)/shard_map/ppermute | solution.py:527
  32.7 2.4 %collective-permute-start.6 = (f32[2,96,256]{2,1,0:T(8,128)S(1)}, f32[2,96,256]{2,1,0:T(8,128)S(1)}, u32[]{:S(2)}, u32[]{:S(2)}) collective-permute-start(f32[2,96,256]{2,1,0:T(8,128)S(1)} %pad_maximum_fusion.refs_0_), channel_id=1, source_target_pairs={{0,2},{1,3},{2,0},{3,1},{4,6},{5,7},{6,4},{7,5},{8,10},{9,11},{10,... | collective-permute-start | bytes 589832 | tf_op jit(solution)/shard_map/ppermute | solution.py:527
  35.2 5.2 %early_first.1 = (f32[512,512]{1,0:T(8,128)S(1)}, f32[304,512]{1,0:T(8,128)S(1)}, f32[304,512]{1,0:T(8,128)S(1)}, f32[608,512]{1,0:T(8,128)S(1)}, f32[304,608]{1,0:T(8,128)S(1)}) custom-call(f32[2,96,256]{2,1,0:T(8,128)S(1)} %pad_maximum_fusion.refs_0_, f32[2,96,256]{2,1,0:T(8,128)S(1)} %pad_maximum_fusion.1.refs_1_, ...), custom_call_target="tpu_custom_call" | custom-call | flops 4000000000 | bytes 4194304 | tf_op jit(solution)/shard_map/early_first/pallas_call | solution.py:335
  40.4 4.0 %collective-permute-done.6.refs_0_ = f32[2,96,256]{2,1,0:T(8,128)S(1)} collective-permute-done((f32[2,96,256]{2,1,0:T(8,128)S(1)}, f32[2,96,256]{2,1,0:T(8,128)S(1)}, u32[]{:S(2)}, u32[]{:S(2)}) %collective-permute-start.6) | collective-permute-done | bytes 196640 | tf_op jit(solution)/shard_map/ppermute | solution.py:527
  44.4 0.8 collective-permute-start.10
  45.2 1.0 %collective-permute-done.10.refs_1_ = f32[2,96,256]{2,1,0:T(8,128)S(1)} collective-permute-done((f32[2,96,256]{2,1,0:T(8,128)S(1)}, f32[2,96,256]{2,1,0:T(8,128)S(1)}, u32[]{:S(2)}, u32[]{:S(2)}) %collective-permute-start.10) | collective-permute-done | bytes 196640 | tf_op jit(solution)/shard_map/ppermute | solution.py:527
  46.3 7.4 %early_second.1 = (f32[512,512]{1,0:T(8,128)S(1)}, f32[304,512]{1,0:T(8,128)S(1)}, f32[304,512]{1,0:T(8,128)S(1)}, f32[608,512]{1,0:T(8,128)S(1)}, f32[304,608]{1,0:T(8,128)S(1)}) custom-call(f32[2,96,256]{2,1,0:T(8,128)S(1)} %collective-permute-done.6.refs_0_, f32[2,96,256]{2,1,0:T(8,128)S(1)} %collective-permute-done.10.refs_1_, ...), custom_call_target="tpu_custom_call" | custom-call | flops 4000000000 | bytes 4194304 | tf_op jit(solution)/shard_map/early_second/pallas_call | solution.py:335
  54.2 1.6 %late_corner.1 = (f32[2,512,512]{2,1,0:T(8,128)S(1)}, bf16[4,512,256]{2,1,0:T(8,128)(2,1)S(1)}, bf16[4,512,256]{2,1,0:T(8,128)(2,1)S(1)}) custom-call(f32[4,96,256]{2,1,0:T(8,128)S(1)} %constant_dynamic-update-slice_fusion.c_ref.own), custom_call_target="tpu_custom_call" | custom-call | flops 1000000000 | bytes 4194304 | tf_op jit(solution)/shard_map/late_corner/pallas_call | solution.py:363
  55.8 25.2 %gram_factor.1 = (f32[297,594]{1,0:T(8,128)}, f32[297,512]{1,0:T(8,128)}) custom-call(s32[2]{0:T(128)S(1)} %pad_add_fusion.scal, f32[4,96,256]{2,1,0:T(8,128)S(1)} %constant_dynamic-update-slice_fusion.c_ref.own, f32[4,96,256]{2,1,0:T(8,128)S(1)} %collective-permute-done.11.oth, bf16[304,224]{1,0:T(8,128)(2,1)S(1)} %get-tuple-element.62.lr.refs_2_, ...), custom_call_target="tpu_custom_call" | custom-call | tf_op jit(solution)/shard_map/gram_factor/pallas_call | solution.py:497
  (25 shorter events, 3.3 us)
Async XLA Ops:
  0.6 1.2 %copy-start = (bf16[96,4096]{1,0:T(8,128)(2,1)S(1)}, bf16[96,4096]{1,0:T(8,128)(2,1)}, u32[]{:S(2)}) copy-start(bf16[96,4096]{1,0:T(8,128)(2,1)} %param.5) | copy-start | bytes 2359300
  5.7 2.4 %collective-permute-start = (f32[96,256]{1,0:T(8,128)S(1)}, f32[96,256]{1,0:T(8,128)S(1)}, u32[]{:S(2)}, u32[]{:S(2)}) collective-permute-start(f32[96,256]{1,0:T(8,128)S(1)} %get-tuple-element.56), channel_id=1, source_target_pairs={{0,8},{8,0},{16,24},{24,16},{32,40},{40,32},{48,56},{56,48},{64,72... | collective-permute-start | bytes 294920 | tf_op jit(solution)/shard_map/ppermute | solution.py:527
  8.1 4.1 %collective-permute-start.1 = (f32[96,256]{1,0:T(8,128)S(1)}, f32[96,256]{1,0:T(8,128)S(1)}, u32[]{:S(2)}, u32[]{:S(2)}) collective-permute-start(f32[96,256]{1,0:T(8,128)S(1)} %add.17), channel_id=1, source_target_pairs={{0,16},{8,40},{16,0},{24,56},{32,48},{40,8},{48,32},{56,24},{64,80... | collective-permute-start | bytes 294920 | tf_op jit(solution)/shard_map/ppermute | solution.py:527
  12.3 3.5 %collective-permute-start.2 = (f32[96,256]{1,0:T(8,128)S(1)}, f32[96,256]{1,0:T(8,128)S(1)}, u32[]{:S(2)}, u32[]{:S(2)}) collective-permute-start(f32[96,256]{1,0:T(8,128)S(1)} %add.18), channel_id=1, source_target_pairs={{0,32},{8,24},{16,48},{24,8},{32,0},{40,56},{48,16},{56,40},{64,96... | collective-permute-start | bytes 294920 | tf_op jit(solution)/shard_map/ppermute | solution.py:527
  15.8 6.0 %collective-permute-start.3 = (f32[96,256]{1,0:T(8,128)S(1)}, f32[96,256]{1,0:T(8,128)S(1)}, u32[]{:S(2)}, u32[]{:S(2)}) collective-permute-start(f32[96,256]{1,0:T(8,128)S(1)} %add.20), channel_id=1, source_target_pairs={{0,64},{8,72},{16,80},{24,88},{32,96},{40,104},{48,112},{56,120},{... | collective-permute-start | bytes 294920 | tf_op jit(solution)/shard_map/ppermute | solution.py:527
  21.8 8.2 %collective-permute-start.5 = (f32[1,96,256]{2,1,0:T(8,128)S(1)}, f32[1,96,256]{2,1,0:T(8,128)S(1)}, u32[]{:S(2)}, u32[]{:S(2)}) collective-permute-start(f32[1,96,256]{2,1,0:T(8,128)S(1)} %add_bitcast_fusion.own), channel_id=1, source_target_pairs={{0,8},{8,0},{16,24},{24,16},{32,40},{40,32},{48,56},{56,48},{64,72... | collective-permute-start | bytes 294920 | tf_op jit(solution)/shard_map/ppermute | solution.py:527
  24.6 5.9 %collective-permute-start.4 = (f32[1,96,256]{2,1,0:T(8,128)S(1)}, f32[1,96,256]{2,1,0:T(8,128)S(1)}, u32[]{:S(2)}, u32[]{:S(2)}) collective-permute-start(f32[1,96,256]{2,1,0:T(8,128)S(1)} %add_bitcast_fusion.own), channel_id=1, source_target_pairs={{0,4},{1,5},{2,6},{3,7},{4,0},{5,1},{6,2},{7,3},{8,12},{9,13},{10,... | collective-permute-start | bytes 294920 | tf_op jit(solution)/shard_map/ppermute | solution.py:527
  30.5 4.6 %collective-permute-start.8 = (f32[1,96,256]{2,1,0:T(8,128)S(1)}, f32[1,96,256]{2,1,0:T(8,128)S(1)}, u32[]{:S(2)}, u32[]{:S(2)}) collective-permute-start(f32[1,96,256]{2,1,0:T(8,128)S(1)} %collective-permute-done.4), channel_id=1, source_target_pairs={{0,8},{8,0},{16,24},{24,16},{32,40},{40,32},{48,56},{56,48},{64,72... | collective-permute-start | bytes 294920 | tf_op jit(solution)/shard_map/ppermute | solution.py:527
  31.4 9.0 %collective-permute-start.7 = (f32[2,96,256]{2,1,0:T(8,128)S(1)}, f32[2,96,256]{2,1,0:T(8,128)S(1)}, u32[]{:S(2)}, u32[]{:S(2)}) collective-permute-start(f32[2,96,256]{2,1,0:T(8,128)S(1)} %pad_maximum_fusion.refs_0_), channel_id=1, source_target_pairs={{0,1},{1,0},{2,3},{3,2},{4,5},{5,4},{6,7},{7,6},{8,9},{9,8},{10,11... | collective-permute-start | bytes 589832 | tf_op jit(solution)/shard_map/ppermute | solution.py:527
  32.7 11.7 %collective-permute-start.6 = (f32[2,96,256]{2,1,0:T(8,128)S(1)}, f32[2,96,256]{2,1,0:T(8,128)S(1)}, u32[]{:S(2)}, u32[]{:S(2)}) collective-permute-start(f32[2,96,256]{2,1,0:T(8,128)S(1)} %pad_maximum_fusion.refs_0_), channel_id=1, source_target_pairs={{0,2},{1,3},{2,0},{3,1},{4,6},{5,7},{6,4},{7,5},{8,10},{9,11},{10,... | collective-permute-start | bytes 589832 | tf_op jit(solution)/shard_map/ppermute | solution.py:527
  44.4 1.9 %collective-permute-start.10 = (f32[2,96,256]{2,1,0:T(8,128)S(1)}, f32[2,96,256]{2,1,0:T(8,128)S(1)}, u32[]{:S(2)}, u32[]{:S(2)}) collective-permute-start(f32[2,96,256]{2,1,0:T(8,128)S(1)} %collective-permute-done.6.refs_0_), channel_id=1, source_target_pairs={{0,8},{8,0},{16,24},{24,16},{32,40},{40,32},{48,56},{56,48},{64,72... | collective-permute-start | bytes 589832 | tf_op jit(solution)/shard_map/ppermute | solution.py:527
  45.2 8.5 %collective-permute-start.9 = (f32[2,96,256]{2,1,0:T(8,128)S(1)}, f32[2,96,256]{2,1,0:T(8,128)S(1)}, u32[]{:S(2)}, u32[]{:S(2)}) collective-permute-start(f32[2,96,256]{2,1,0:T(8,128)S(1)} %collective-permute-done.6.refs_0_), channel_id=1, source_target_pairs={{0,1},{1,0},{2,3},{3,2},{4,5},{5,4},{6,7},{7,6},{8,9},{9,8},{10,11... | collective-permute-start | bytes 589832 | tf_op jit(solution)/shard_map/ppermute | solution.py:527
  53.7 2.0 %collective-permute-start.11 = (f32[4,96,256]{2,1,0:T(8,128)S(1)}, f32[4,96,256]{2,1,0:T(8,128)S(1)}, u32[]{:S(2)}, u32[]{:S(2)}) collective-permute-start(f32[4,96,256]{2,1,0:T(8,128)S(1)} %constant_dynamic-update-slice_fusion.c_ref.own), channel_id=1, source_target_pairs={{0,8},{8,0},{16,24},{24,16},{32,40},{40,32},{48,56},{56,48},{64,72... | collective-permute-start | bytes 1179656 | tf_op jit(solution)/shard_map/ppermute | solution.py:527
